TPU v7x, 32 devices: a whole 2x2x4 slice. The times are simulated.
32 devices in a mesh: group: 4 (over y, core), dp: 8 (over z, x).
Axes of the slice: x: 2, y: 2, z: 4, core: 2. Of those that a mesh axis runs over, the one named last changes fastest.
Arguments:
- table: bfloat16 [16384, 1024], P(('group', 'dp')), may hold values from -6 to 6
- accum: float32 [16384], P(('group', 'dp')), may hold values from 0.05 to 5
- pair_block: int32 [1024], P(('group', 'dp')), may hold values from 0 to 127, as said below
- pair_protein: int32 [1024], P(('group', 'dp')), may hold values from 0 to 127, as said below
- pair_weight: bfloat16 [1024, 128], P(('group', 'dp')), may hold values from 0 to 1, as said below
- w_hidden: bfloat16 [1024, 1024], replicated, may hold values from -0.1875 to 0.1875
- hidden_cot: bfloat16 [128, 1024], P(('group', 'dp')), may hold values from -6 to 6
Outputs:
- new_table: bfloat16 [16384, 1024], P(('group', 'dp'))
- new_accum: float32 [16384], P(('group', 'dp'))
Inputs may be any that keep to these rules, and one draw needn't show every extreme that they name: `pair_block`: the owner of block b is device b // 4 along group+dp. Of one device's 32 pairs at most 2 name blocks of one owner; every device reaches 2 for some owner, and some owner receives 2 pairs from every device. `pair_protein`: A device's pairs name only that device's proteins (index // 4 is the device's index along group+dp), each of them at least once. `pair_weight`: Nonnegative; every pair has at least one positive weight.
All inputs are finite; a program needn't handle non-finite values.
Results may differ from a plain program's by a relative error of at most 0.001.
Values may be sent and summed in bfloat16 or wider, within the bound.
A program may use at most 64 MiB of HBM per device.

v0:
```python
import jax
import jax.numpy as jnp
from jax import lax
from jax.sharding import PartitionSpec as P

CAP = 2


def mlp_grad(bag, w_hidden, hidden_cot):
    inv = lax.rsqrt(jnp.mean(bag * bag, axis=-1, keepdims=True) + 1e-06)
    unit = bag * inv
    unit_b = unit.astype(jnp.bfloat16)
    pre = jnp.dot(unit_b, w_hidden, preferred_element_type=jnp.float32)
    sig = jax.nn.sigmoid(pre)
    dpre = (hidden_cot.astype(jnp.float32) * sig * (1.0 + pre * (1.0 - sig))).astype(jnp.bfloat16)
    dunit = lax.dot_general(
        dpre, w_hidden, (((1,), (1,)), ((), ())), preferred_element_type=jnp.float32
    )
    dbag = (dunit - unit * jnp.mean(dunit * unit, axis=-1, keepdims=True)) * inv
    return dbag.astype(jnp.bfloat16)


def per_device(table, accum, pair_block, pair_protein, pair_weight, w_hidden, hidden_cot):
    n_group = lax.axis_size("group")
    n_dp = lax.axis_size("dp")
    devices = n_group * n_dp
    rows_dev, width = table.shape
    block_rows = pair_weight.shape[1]
    blocks_dev = rows_dev // block_rows
    pairs = pair_block.shape[0]
    proteins = hidden_cot.shape[0]
    slots = CAP * devices
    device_id = lax.axis_index("group") * n_dp + lax.axis_index("dp")
    owner = pair_block // blocks_dev
    local_block = pair_block % blocks_dev
    local_prot = pair_protein - device_id * proteins
    positions = jnp.arange(pairs, dtype=jnp.int32)
    earlier = (owner[:, None] == owner[None, :]) & (positions[None, :] < positions[:, None])
    rank = jnp.sum(earlier.astype(jnp.int32), axis=1)
    slot = owner * CAP + rank
    place = slot[None, :] == jnp.arange(slots, dtype=jnp.int32)[:, None]
    place_b = place.astype(jnp.bfloat16)
    send_w = jnp.dot(place_b, pair_weight, preferred_element_type=jnp.float32).astype(jnp.bfloat16)
    send_blk = jnp.max(jnp.where(place, local_block[None, :], -1), axis=1)
    send_pid = jnp.max(jnp.where(place, pair_protein[None, :], -1), axis=1)
    got_w, got_blk, got_pid = (
        lax.all_to_all(
            lax.all_to_all(
                send_w.reshape(n_group, n_dp, CAP, block_rows),
                "group",
                split_axis=0,
                concat_axis=0,
                tiled=True,
            ),
            "dp",
            split_axis=1,
            concat_axis=1,
            tiled=True,
        ),
        lax.all_to_all(
            lax.all_to_all(
                send_blk.reshape(n_group, n_dp, CAP),
                "group",
                split_axis=0,
                concat_axis=0,
                tiled=True,
            ),
            "dp",
            split_axis=1,
            concat_axis=1,
            tiled=True,
        ),
        lax.all_to_all(
            lax.all_to_all(
                send_pid.reshape(n_group, n_dp, CAP),
                "group",
                split_axis=0,
                concat_axis=0,
                tiled=True,
            ),
            "dp",
            split_axis=1,
            concat_axis=1,
            tiled=True,
        ),
    )
    got_w = got_w.reshape(slots, block_rows)
    got_blk = got_blk.reshape(slots)
    got_pid = got_pid.reshape(slots)
    hit = got_blk[:, None, None] == jnp.arange(blocks_dev, dtype=jnp.int32)[None, :, None]
    dense = jnp.where(hit, got_w[:, None, :], jnp.zeros((), jnp.bfloat16)).reshape(slots, rows_dev)
    partial_value = jnp.dot(dense, table, preferred_element_type=jnp.float32).astype(jnp.bfloat16)
    returned = lax.all_to_all(
        lax.all_to_all(
            partial_value.reshape(n_group, n_dp, CAP, width),
            "group",
            split_axis=0,
            concat_axis=0,
            tiled=True,
        ),
        "dp",
        split_axis=1,
        concat_axis=1,
        tiled=True,
    )
    returned = returned.reshape(slots, width)
    prot_onehot = (local_prot[None, :] == jnp.arange(proteins, dtype=jnp.int32)[:, None]).astype(
        jnp.bfloat16
    )
    prot_slot = lax.dot_general(
        prot_onehot, place_b, (((1,), (1,)), ((), ())), preferred_element_type=jnp.float32
    ).astype(jnp.bfloat16)
    bag = jnp.dot(prot_slot, returned, preferred_element_type=jnp.float32)
    dbag = mlp_grad(bag, w_hidden, hidden_cot)
    every_grad = lax.all_gather(dbag, ("group", "dp"), axis=0, tiled=True)
    got_grad = jnp.take(every_grad, jnp.maximum(got_pid, 0), axis=0)
    grad = lax.dot_general(
        dense, got_grad, (((0,), (0,)), ((), ())), preferred_element_type=jnp.float32
    )
    acc_new = accum + jnp.mean(grad * grad, axis=-1)
    rows_new = table.astype(jnp.float32) - 0.3 * grad / (jnp.sqrt(acc_new)[:, None] + 1e-08)
    return (rows_new.astype(jnp.bfloat16), acc_new)


def solution(mesh):
    in_specs = (
        P(("group", "dp"), None),
        P(("group", "dp")),
        P(("group", "dp")),
        P(("group", "dp")),
        P(("group", "dp"), None),
        P(),
        P(("group", "dp"), None),
    )
    out_specs = (P(("group", "dp"), None), P(("group", "dp")))
    return jax.shard_map(
        per_device, mesh=mesh, in_specs=in_specs, out_specs=out_specs, check_vma=False
    )
```

profile of v0, /device:TPU:0, one launch (start us, length us, event | category | flops | bytes accessed | tf_op | source)
XLA Modules:
  0.0 157.5 jit_solution(832334423943689691)
XLA Ops:
  0.7 0.8 and_select_fusion
  1.5 0.2 convert_reduce_fusion
  1.7 0.8 select_reduce_fusion
  2.4 0.1 reshape.96
  2.5 0.7 copy.51
  3.2 4.2 %all-to-all-start = ((s32[4,8,2]{1,2,0:T(2,128)}), s32[4,8,2]{1,2,0:T(2,128)S(1)}, u32[]{:S(2)}, u32[]{:S(2)}) async-start(s32[4,8,2]{1,2,0:T(2,128)} %copy.51), calls=%async_computation | async-start | bytes 8192 | tf_op jit(solution)/shard_map/all_to_all | solution.py:61
  7.4 0.1 reshape.98
  7.5 0.7 copy.56
  8.2 3.0 %all-to-all-done = s32[4,8,2]{1,2,0:T(2,128)S(1)} async-done(((s32[4,8,2]{1,2,0:T(2,128)}), s32[4,8,2]{1,2,0:T(2,128)S(1)}, u32[]{:S(2)}, u32[]{:S(2)}) %all-to-all-start) | async-done | bytes 288 | tf_op jit(solution)/shard_map/all_to_all | solution.py:61
  11.2 3.2 %all-to-all-start.4 = ((s32[4,8,2]{1,2,0:T(2,128)}), s32[4,8,2]{1,2,0:T(2,128)S(1)}, u32[]{:S(2)}, u32[]{:S(2)}) async-start(s32[4,8,2]{1,2,0:T(2,128)} %copy.56), calls=%async_computation.4 | async-start | bytes 8192 | tf_op jit(solution)/shard_map/all_to_all | solution.py:74
  14.5 0.7 copy.52
  15.1 3.1 %all-to-all-done.4 = s32[4,8,2]{1,2,0:T(2,128)S(1)} async-done(((s32[4,8,2]{1,2,0:T(2,128)}), s32[4,8,2]{1,2,0:T(2,128)S(1)}, u32[]{:S(2)}, u32[]{:S(2)}) %all-to-all-start.4) | async-done | bytes 288 | tf_op jit(solution)/shard_map/all_to_all | solution.py:74
  18.2 6.2 %all-to-all-start.1 = ((s32[4,8,2]{0,2,1:T(2,128)}), s32[4,8,2]{0,2,1:T(2,128)S(1)}, u32[]{:S(2)}, u32[]{:S(2)}) async-start(s32[4,8,2]{0,2,1:T(2,128)} %copy.52), calls=%async_computation.1 | async-start | bytes 16384 | tf_op jit(solution)/shard_map/all_to_all | solution.py:60
  24.4 1.6 convolution_convert_fusion.1
  26.0 4.9 %all-to-all-done.1 = s32[4,8,2]{0,2,1:T(2,128)S(1)} async-done(((s32[4,8,2]{0,2,1:T(2,128)}), s32[4,8,2]{0,2,1:T(2,128)S(1)}, u32[]{:S(2)}, u32[]{:S(2)}) %all-to-all-start.1) | async-done | bytes 288 | tf_op jit(solution)/shard_map/all_to_all | solution.py:60
  30.9 3.3 %all-to-all-start.2 = ((bf16[4,8,2,128]{3,2,1,0:T(2,128)(2,1)}), bf16[4,8,2,128]{3,2,1,0:T(2,128)(2,1)S(1)}, u32[]{:S(2)}, u32[]{:S(2)}) async-start(bf16[4,8,2,128]{3,2,1,0:T(2,128)(2,1)} %bitcast), calls=%async_computation.2 | async-start | bytes 32768 | tf_op jit(solution)/shard_map/all_to_all | solution.py:48
  34.2 0.7 copy.57
  34.9 3.1 %all-to-all-done.2 = bf16[4,8,2,128]{3,2,1,0:T(2,128)(2,1)S(1)} async-done(((bf16[4,8,2,128]{3,2,1,0:T(2,128)(2,1)}), bf16[4,8,2,128]{3,2,1,0:T(2,128)(2,1)S(1)}, u32[]{:S(2)}, u32[]{:S(2)}) %all-to-all-start.2) | async-done | bytes 16416 | tf_op jit(solution)/shard_map/all_to_all | solution.py:48
  38.0 3.3 %all-to-all-start.5 = ((s32[4,8,2]{0,2,1:T(2,128)}), s32[4,8,2]{0,2,1:T(2,128)S(1)}, u32[]{:S(2)}, u32[]{:S(2)}) async-start(s32[4,8,2]{0,2,1:T(2,128)} %copy.57), calls=%async_computation.5 | async-start | bytes 16384 | tf_op jit(solution)/shard_map/all_to_all | solution.py:73
  41.4 0.7 broadcast_subtract_fusion
  42.0 0.1 copy.53
  42.2 0.1 eq.67
  42.3 0.6 copy.54
  42.9 4.9 %all-to-all-done.5 = s32[4,8,2]{0,2,1:T(2,128)S(1)} async-done(((s32[4,8,2]{0,2,1:T(2,128)}), s32[4,8,2]{0,2,1:T(2,128)S(1)}, u32[]{:S(2)}, u32[]{:S(2)}) %all-to-all-start.5) | async-done | bytes 288 | tf_op jit(solution)/shard_map/all_to_all | solution.py:73
  47.8 3.3 %all-to-all-start.3 = ((bf16[4,8,2,128]{3,2,0,1:T(2,128)(2,1)}), bf16[4,8,2,128]{3,2,0,1:T(2,128)(2,1)S(1)}, u32[]{:S(2)}, u32[]{:S(2)}) async-start(bf16[4,8,2,128]{3,2,0,1:T(2,128)(2,1)} %copy.54), calls=%async_computation.3 | async-start | bytes 32768 | tf_op jit(solution)/shard_map/all_to_all | solution.py:47
  51.2 0.1 copy.58
  51.3 6.3 %all-to-all-done.3 = bf16[4,8,2,128]{3,2,0,1:T(2,128)(2,1)S(1)} async-done(((bf16[4,8,2,128]{3,2,0,1:T(2,128)(2,1)}), bf16[4,8,2,128]{3,2,0,1:T(2,128)(2,1)S(1)}, u32[]{:S(2)}, u32[]{:S(2)}) %all-to-all-start.3) | async-done | bytes 16416 | tf_op jit(solution)/shard_map/all_to_all | solution.py:47
  57.7 0.1 broadcast_select_fusion
  57.8 1.5 convolution_convert_fusion
  59.4 0.7 reshape.99
  60.1 3.3 %all-to-all-start.6 = ((bf16[4,8,2,1024]{3,2,1,0:T(2,128)(2,1)}), bf16[4,8,2,1024]{3,2,1,0:T(2,128)(2,1)S(1)}, u32[]{:S(2)}, u32[]{:S(2)}) async-start(bf16[4,8,2,1024]{3,2,1,0:T(2,128)(2,1)} %reshape.99), calls=%async_computation.6 | async-start | bytes 262144 | tf_op jit(solution)/shard_map/all_to_all | solution.py:94
  63.4 0.1 copy.59
  63.5 0.1 le.16
  63.6 4.4 %all-to-all-done.6 = bf16[4,8,2,1024]{3,2,1,0:T(2,128)(2,1)S(1)} async-done(((bf16[4,8,2,1024]{3,2,1,0:T(2,128)(2,1)}), bf16[4,8,2,1024]{3,2,1,0:T(2,128)(2,1)S(1)}, u32[]{:S(2)}, u32[]{:S(2)}) %all-to-all-start.6) | async-done | bytes 131104 | tf_op jit(solution)/shard_map/all_to_all | solution.py:94
  68.0 0.8 copy.60
  68.8 3.4 %all-to-all-start.7 = ((bf16[4,8,2,1024]{3,2,0,1:T(2,128)(2,1)}), bf16[4,8,2,1024]{3,2,0,1:T(2,128)(2,1)S(1)}, u32[]{:S(2)}, u32[]{:S(2)}) async-start(bf16[4,8,2,1024]{3,2,0,1:T(2,128)(2,1)} %copy.60), calls=%async_computation.7 | async-start | bytes 262144 | tf_op jit(solution)/shard_map/all_to_all | solution.py:93
  72.1 0.1 copy.62
  72.2 0.1 reshape.103
  72.4 7.0 %all-to-all-done.7 = bf16[4,8,2,1024]{3,2,0,1:T(2,128)(2,1)S(1)} async-done(((bf16[4,8,2,1024]{3,2,0,1:T(2,128)(2,1)}), bf16[4,8,2,1024]{3,2,0,1:T(2,128)(2,1)S(1)}, u32[]{:S(2)}, u32[]{:S(2)}) %all-to-all-start.7) | async-done | bytes 131104 | tf_op jit(solution)/shard_map/all_to_all | solution.py:93
  79.4 0.1 copy.61
  79.6 0.4 multiply_reduce_fusion.2
  80.0 1.1 multiply_reduce_fusion.1
  81.2 70.3 %all-gather = bf16[32,4,1024]{2,1,0:T(4,128)(2,1)} all-gather(bf16[1,4,1024]{2,1,0:T(4,128)(2,1)S(1)} %fusion.12), channel_id=1, replica_groups=mesh['group'=4,'dp'=8] {'group','dp'}, dimensions={0}, use_global_device_ids=true | all-gather | bytes 270336 | tf_op jit(solution)/shard_map/all_gather | solution.py:115
  151.5 1.0 reshape.111
  152.5 1.4 gather_fusion
  153.9 1.5 multiply_reduce_fusion
  155.3 0.6 sqrt_add_fusion
  155.9 1.6 subtract_convert_fusion
  (18 shorter events, 0.3 us)
Async XLA Ops:
  0.6 79.4 %copy-start = (bf16[1024,1024]{1,0:T(8,128)(2,1)S(1)}, bf16[1024,1024]{1,0:T(8,128)(2,1)}, u32[]{:S(2)}) copy-start(bf16[1024,1024]{1,0:T(8,128)(2,1)} %param.12) | copy-start | bytes 6291460
  0.6 79.4 %copy-start.2 = (bf16[4,1024]{1,0:T(4,128)(2,1)S(1)}, bf16[4,1024]{1,0:T(4,128)(2,1)}, u32[]{:S(2)}) copy-start(bf16[4,1024]{1,0:T(4,128)(2,1)} %param.13) | copy-start | bytes 24580
  3.2 8.0 %all-to-all-start = ((s32[4,8,2]{1,2,0:T(2,128)}), s32[4,8,2]{1,2,0:T(2,128)S(1)}, u32[]{:S(2)}, u32[]{:S(2)}) async-start(s32[4,8,2]{1,2,0:T(2,128)} %copy.51), calls=%async_computation | async-start | bytes 8192 | tf_op jit(solution)/shard_map/all_to_all | solution.py:61
  11.2 7.0 %all-to-all-start.4 = ((s32[4,8,2]{1,2,0:T(2,128)}), s32[4,8,2]{1,2,0:T(2,128)S(1)}, u32[]{:S(2)}, u32[]{:S(2)}) async-start(s32[4,8,2]{1,2,0:T(2,128)} %copy.56), calls=%async_computation.4 | async-start | bytes 8192 | tf_op jit(solution)/shard_map/all_to_all | solution.py:74
  18.2 12.7 %all-to-all-start.1 = ((s32[4,8,2]{0,2,1:T(2,128)}), s32[4,8,2]{0,2,1:T(2,128)S(1)}, u32[]{:S(2)}, u32[]{:S(2)}) async-start(s32[4,8,2]{0,2,1:T(2,128)} %copy.52), calls=%async_computation.1 | async-start | bytes 16384 | tf_op jit(solution)/shard_map/all_to_all | solution.py:60
  30.9 7.1 %all-to-all-start.2 = ((bf16[4,8,2,128]{3,2,1,0:T(2,128)(2,1)}), bf16[4,8,2,128]{3,2,1,0:T(2,128)(2,1)S(1)}, u32[]{:S(2)}, u32[]{:S(2)}) async-start(bf16[4,8,2,128]{3,2,1,0:T(2,128)(2,1)} %bitcast), calls=%async_computation.2 | async-start | bytes 32768 | tf_op jit(solution)/shard_map/all_to_all | solution.py:48
  38.0 9.8 %all-to-all-start.5 = ((s32[4,8,2]{0,2,1:T(2,128)}), s32[4,8,2]{0,2,1:T(2,128)S(1)}, u32[]{:S(2)}, u32[]{:S(2)}) async-start(s32[4,8,2]{0,2,1:T(2,128)} %copy.57), calls=%async_computation.5 | async-start | bytes 16384 | tf_op jit(solution)/shard_map/all_to_all | solution.py:73
  47.8 9.9 %all-to-all-start.3 = ((bf16[4,8,2,128]{3,2,0,1:T(2,128)(2,1)}), bf16[4,8,2,128]{3,2,0,1:T(2,128)(2,1)S(1)}, u32[]{:S(2)}, u32[]{:S(2)}) async-start(bf16[4,8,2,128]{3,2,0,1:T(2,128)(2,1)} %copy.54), calls=%async_computation.3 | async-start | bytes 32768 | tf_op jit(solution)/shard_map/all_to_all | solution.py:47
  60.1 7.9 %all-to-all-start.6 = ((bf16[4,8,2,1024]{3,2,1,0:T(2,128)(2,1)}), bf16[4,8,2,1024]{3,2,1,0:T(2,128)(2,1)S(1)}, u32[]{:S(2)}, u32[]{:S(2)}) async-start(bf16[4,8,2,1024]{3,2,1,0:T(2,128)(2,1)} %reshape.99), calls=%async_computation.6 | async-start | bytes 262144 | tf_op jit(solution)/shard_map/all_to_all | solution.py:94
  68.8 10.7 %all-to-all-start.7 = ((bf16[4,8,2,1024]{3,2,0,1:T(2,128)(2,1)}), bf16[4,8,2,1024]{3,2,0,1:T(2,128)(2,1)S(1)}, u32[]{:S(2)}, u32[]{:S(2)}) async-start(bf16[4,8,2,1024]{3,2,0,1:T(2,128)(2,1)} %copy.60), calls=%async_computation.7 | async-start | bytes 262144 | tf_op jit(solution)/shard_map/all_to_all | solution.py:93
  81.2 74.1 %copy-start.3 = (f32[512]{0:T(512)S(1)}, f32[512]{0:T(512)}, u32[]{:S(2)}) copy-start(f32[512]{0:T(512)} %param.8) | copy-start | bytes 6148
  81.2 74.7 %copy-start.1 = (bf16[512,1024]{1,0:T(8,128)(2,1)S(1)}, bf16[512,1024]{1,0:T(8,128)(2,1)}, u32[]{:S(2)}) copy-start(bf16[512,1024]{1,0:T(8,128)(2,1)} %param.7) | copy-start | bytes 3145732
where the time goes:
time: 158 us; the launch traced here: 157 us
  blocking collectives  70.3 us (44%)
  waiting for transfers between devices  36.8 us (23%)
  starting transfers between devices  30.3 us (19%)
  local copies, waits for them, and re-layouts  8.33 us (5%)
  matrix products  6.05 us (4%)
  other arithmetic  4.89 us (3%)
    all_gather x1, blocking collectives, per_device(): every_grad = lax.all_gather(dbag, ('group', 'dp'), axis=0, tiled=True)  70.3 us
    all_to_all x1, waiting for transfers between devices, per_device(): lax.all_to_all(lax.all_to_all(partial_value.reshape(n_group, n_dp, CAP, w...  7.05 us
    all_to_all x1, waiting for transfers between devices, per_device(): lax.all_to_all(lax.all_to_all(send_w.reshape(n_group, n_dp, CAP, block_ro...  6.35 us
    all_to_all x1, starting transfers between devices, per_device(): lax.all_to_all(lax.all_to_all(send_blk.reshape(n_group, n_dp, CAP), 'grou...  6.24 us
    all_to_all x1, waiting for transfers between devices, per_device(): lax.all_to_all(lax.all_to_all(send_blk.reshape(n_group, n_dp, CAP), 'grou...  4.94 us
    all_to_all x1, waiting for transfers between devices, per_device(): lax.all_to_all(lax.all_to_all(send_pid.reshape(n_group, n_dp, CAP), 'grou...  4.92 us
    all_to_all x1, waiting for transfers between devices, per_device(): lax.all_to_all(partial_value.reshape(n_group, n_dp, CAP, width), 'group',...  4.36 us
    all_to_all x1, starting transfers between devices, per_device(): lax.all_to_all(send_blk.reshape(n_group, n_dp, CAP), 'group', split_axis=...  4.24 us
  transfers between devices with their start and end apart: 8, of which 8 were waited for; matrix products, arithmetic and copies ran while one was open for 4% of the time, Pallas kernels for 0%

commit v1 on v0

v1 whole, which is shorter than its diff:
```python
import functools

import jax
import jax.numpy as jnp
from jax import lax
from jax.experimental import pallas as pl
from jax.experimental.pallas import tpu as pltpu
from jax.sharding import PartitionSpec as P

CAP = 2
LANES = 128
TOGETHER = 16
PAD = 8
MESH = pl.DeviceIdType.MESH
BF = jnp.bfloat16
F32 = jnp.float32


def dot(a, b):
    return jnp.dot(a, b, preferred_element_type=F32)


def dot_nt(a, b):
    return lax.dot_general(a, b, (((1,), (1,)), ((), ())), preferred_element_type=F32)


def iota(shape, dim):
    return lax.broadcasted_iota(jnp.int32, shape, dim)


def ones_where(mask):
    return jnp.where(mask, 1.0, 0.0).astype(BF)


def kernel(
    n_group,
    n_dp,
    blk_ref,
    prot_ref,
    w_ref,
    cot_ref,
    accum_ref,
    table_hbm,
    hid_hbm,
    out_hbm,
    acc_ref,
    table,
    hid,
    rows_out,
    send_w,
    got_w,
    send_part,
    got_part,
    send_grad,
    got_grad,
    dense,
    dense_t,
    gathered,
    pick,
    pick_t,
    sends,
    recvs,
    loads,
    stores,
):
    n = n_group * n_dp
    me = lax.axis_index("group") * n_dp + lax.axis_index("dp")
    load_table = pltpu.make_async_copy(table_hbm, table, loads.at[0])
    load_hid = pltpu.make_async_copy(hid_hbm, hid, loads.at[1])
    load_table.start()
    load_hid.start()

    def where_is(t):
        return (lax.div(t, n_dp), lax.rem(t, n_dp))

    barrier = pltpu.get_barrier_semaphore()

    def greet(i, carry):
        t = lax.rem(me + i, n)
        pl.semaphore_signal(barrier, inc=1, device_id=where_is(t), device_id_type=MESH)
        return carry

    lax.fori_loop(1, n, greet, 0)

    def exchange(send, got, phase):
        def start(i, carry):
            t = lax.rem(me + i, n)
            pltpu.make_async_remote_copy(
                src_ref=send.at[t],
                dst_ref=got.at[me],
                send_sem=sends.at[phase],
                recv_sem=recvs.at[phase],
                device_id=where_is(t),
                device_id_type=MESH,
            ).start()
            return carry

        lax.fori_loop(1, n, start, 0)
        got[me] = send[me]

    others = pl.ds(0, n - 1)

    def arrived(got, phase):
        pltpu.make_async_copy(got.at[others], got.at[others], recvs.at[phase]).wait()

    def left(send, phase):
        pltpu.make_async_copy(send.at[others], send.at[others], sends.at[phase]).wait()

    width = table.shape[1]
    block_rows = w_ref.shape[1]
    blocks = table.shape[0] // block_rows
    chunks = width // LANES
    proteins = cot_ref.shape[0]
    pairs = w_ref.shape[0]
    tile = chunks * CAP
    slots = n * CAP
    step = min(TOGETHER, n)
    groups = n // step
    rows = step * tile
    few = groups <= 4

    def each(body):
        if few:
            for g in range(groups):
                body(g)
        else:
            lax.fori_loop(0, groups, lambda g, c: (body(g), c)[1], 0)

    def at(g, size):
        return pl.ds(g * size, size) if few else pl.ds(pl.multiple_of(g * size, size), size)

    blk = blk_ref[...]
    owner = lax.div(blk, blocks)
    local = lax.rem(blk, blocks)
    local_prot = prot_ref[...] - me * proteins
    square = (pairs, pairs)
    from_row, from_col = iota(square, 0), iota(square, 1)
    owner_f = owner.astype(F32)
    owner_col = jnp.sum(jnp.where(from_row == from_col, owner_f, 0.0), axis=1, keepdims=True)
    earlier = (owner_col == owner_f) & (from_row < from_col)
    rank = jnp.sum(jnp.where(earlier, 1.0, 0.0), axis=0, keepdims=True)
    slot = owner * CAP + rank.astype(jnp.int32)

    place_rows = iota((rows, pairs), 0)
    place_c = lax.rem(place_rows, tile) // CAP
    place_slot = (place_rows // tile) * CAP + lax.rem(place_rows, CAP)
    for_prot = ones_where(iota((chunks * PAD, pairs), 0) % PAD == local_prot)
    same_c = iota((chunks * PAD, rows), 0) // PAD == (iota((chunks * PAD, rows), 1) % tile) // CAP
    same_c_t = iota((rows, chunks * PAD), 1) // PAD == (iota((rows, chunks * PAD), 0) % tile) // CAP
    weights = w_ref[...]

    def place_of(g):
        return place_slot + g * (step * CAP) == slot

    def make_w(g):
        place = place_of(g) & (place_c == local)
        send_w[at(g, step)] = dot(ones_where(place), weights).astype(BF).reshape(step, tile, LANES)

    each(make_w)
    pl.semaphore_wait(barrier, n - 1)
    exchange(send_w, got_w, 0)

    def make_pick(g):
        place = ones_where(place_of(g))
        pick[g] = jnp.where(same_c, dot_nt(for_prot, place), 0.0).astype(BF)
        pick_t[at(g, rows), :] = jnp.where(same_c_t, dot_nt(place, for_prot), 0.0).astype(BF)

    each(make_pick)

    to_r, to_c = iota((rows, rows), 0), iota((rows, rows), 1)
    stacked = step * CAP
    r_c, r_d, r_k = to_r // stacked, (to_r % stacked) // CAP, to_r % CAP
    unpack = ones_where(to_c == r_d * tile + r_c * CAP + r_k)
    t_c, t_d, t_k = to_c // stacked, (to_c % stacked) // CAP, to_c % CAP
    pack = ones_where(to_r == t_d * tile + t_c * CAP + t_k)

    def unpacked(got, g, count):
        flat = got[at(g, step)].reshape(rows, LANES)
        high = dot(unpack[: count * stacked], flat)
        return jnp.concatenate(
            [high[c * stacked : (c + 1) * stacked] for c in range(count)], axis=1
        )

    arrived(got_w, 0)

    def make_dense(g):
        dense[at(g, stacked), :] = unpacked(got_w, g, blocks * block_rows // LANES).astype(BF)

    each(make_dense)
    load_table.wait()
    big = min(slots, 256)
    per_big = big // stacked

    def make_part(h):
        some = dense[pl.ds(h * big if few else pl.multiple_of(h * big, big), big), :]
        part = dot(some, table[...]).astype(BF)
        for j in range(per_big):
            own = part[j * stacked : (j + 1) * stacked]
            stack = jnp.concatenate(
                [own[:, c * LANES : (c + 1) * LANES] for c in range(chunks)], axis=0
            )
            send_part[at(h * per_big + j, step)] = (
                dot(pack, stack).astype(BF).reshape(step, tile, LANES)
            )

    if few:
        for h in range(slots // big):
            make_part(h)
    else:
        lax.fori_loop(0, slots // big, lambda h, c: (make_part(h), c)[1], 0)
    exchange(send_part, got_part, 1)

    dense_t[...] = dense[...].astype(F32).T.astype(BF)
    load_hid.wait()
    arrived(got_part, 1)

    def bag_of(g):
        return dot(pick[g], got_part[at(g, step)].reshape(rows, LANES))

    if few:
        stack = sum(bag_of(g) for g in range(groups))
    else:
        stack = lax.fori_loop(
            0, groups, lambda g, c: c + bag_of(g), jnp.zeros((chunks * PAD, LANES), F32)
        )
    bag = jnp.concatenate([stack[c * PAD : (c + 1) * PAD] for c in range(chunks)], axis=1)
    cot = cot_ref[...].astype(F32)
    cot = jnp.concatenate([cot, jnp.zeros((PAD - proteins, cot.shape[1]), F32)], axis=0)
    inv = lax.rsqrt(jnp.mean(bag * bag, axis=-1, keepdims=True) + 1e-06)
    unit = bag * inv
    pre = dot(unit.astype(BF), hid[...])
    sig = jax.nn.sigmoid(pre)
    dpre = (cot * sig * (1.0 + pre * (1.0 - sig))).astype(BF)
    dunit = dot_nt(dpre, hid[...])
    dbag = (dunit - unit * jnp.mean(dunit * unit, axis=-1, keepdims=True)) * inv
    dstack = jnp.concatenate(
        [dbag[:, c * LANES : (c + 1) * LANES] for c in range(chunks)], axis=0
    ).astype(BF)

    def make_grad(g):
        send_grad[at(g, step)] = (
            dot(pick_t[at(g, rows), :], dstack).astype(BF).reshape(step, tile, LANES)
        )

    each(make_grad)
    exchange(send_grad, got_grad, 2)
    left(send_w, 0)
    left(send_part, 1)
    arrived(got_grad, 2)

    def make_gathered(g):
        gathered[at(g, stacked), :] = unpacked(got_grad, g, chunks).astype(BF)

    each(make_gathered)
    diagonal = iota((block_rows, block_rows), 0) == iota((block_rows, block_rows), 1)
    writes = []
    for b in range(blocks):
        some = pl.ds(b * block_rows, block_rows)
        grad = dot(dense_t[some, :], gathered[...])
        mean = jnp.mean(grad * grad, axis=-1, keepdims=True)
        old = jnp.sum(jnp.where(diagonal, accum_ref[b : b + 1, :], 0.0), axis=1, keepdims=True)
        new = old + mean
        scale = 0.3 / (jnp.sqrt(new) + 1e-08)
        rows_out[some, :] = (table[some, :].astype(F32) - grad * scale).astype(BF)
        write = pltpu.make_async_copy(rows_out.at[some], out_hbm.at[some], stores.at[b])
        write.start()
        writes.append(write)
        acc_ref[b : b + 1, :] = jnp.sum(jnp.where(diagonal, new, 0.0), axis=0, keepdims=True)
    left(send_grad, 2)
    for write in writes:
        write.wait()


def per_device(table, accum, pair_block, pair_protein, pair_weight, w_hidden, hidden_cot):
    n_group = lax.axis_size("group")
    n_dp = lax.axis_size("dp")
    n = n_group * n_dp
    rows_dev, width = table.shape
    pairs, block_rows = pair_weight.shape
    blocks = rows_dev // block_rows
    tile = (width // LANES) * CAP
    slots = n * CAP
    step = min(TOGETHER, n)
    vmem = pl.BlockSpec(memory_space=pltpu.VMEM)
    hbm = pl.BlockSpec(memory_space=pl.ANY)
    tiles = pltpu.VMEM((n, tile, LANES), BF)
    stack = (width // LANES) * PAD
    new_table, new_accum = pl.pallas_call(
        functools.partial(kernel, n_group, n_dp),
        out_shape=(
            jax.ShapeDtypeStruct(table.shape, BF),
            jax.ShapeDtypeStruct((blocks, block_rows), F32),
        ),
        in_specs=[vmem] * 5 + [hbm] * 2,
        out_specs=(hbm, vmem),
        scratch_shapes=[
            pltpu.VMEM(table.shape, BF),
            pltpu.VMEM(w_hidden.shape, BF),
            pltpu.VMEM(table.shape, BF),
            tiles,
            tiles,
            tiles,
            tiles,
            tiles,
            tiles,
            pltpu.VMEM((slots, rows_dev), BF),
            pltpu.VMEM((rows_dev, slots), BF),
            pltpu.VMEM((slots, width), BF),
            pltpu.VMEM((n // step, stack, step * tile), BF),
            pltpu.VMEM((n * tile, stack), BF),
            pltpu.SemaphoreType.DMA((3,)),
            pltpu.SemaphoreType.DMA((3,)),
            pltpu.SemaphoreType.DMA((2,)),
            pltpu.SemaphoreType.DMA((blocks,)),
        ],
        compiler_params=pltpu.CompilerParams(
            collective_id=0, has_side_effects=True, vmem_limit_bytes=48 * 1024 * 1024
        ),
        name="bags",
    )(
        pair_block.reshape(1, pairs),
        pair_protein.reshape(1, pairs),
        pair_weight,
        hidden_cot,
        accum.reshape(blocks, block_rows),
        table,
        w_hidden,
    )
    return new_table, new_accum.reshape(rows_dev)


def solution(mesh):
    in_specs = (
        P(("group", "dp"), None),
        P(("group", "dp")),
        P(("group", "dp")),
        P(("group", "dp")),
        P(("group", "dp"), None),
        P(),
        P(("group", "dp"), None),
    )
    out_specs = (P(("group", "dp"), None), P(("group", "dp")))
    return jax.shard_map(
        per_device, mesh=mesh, in_specs=in_specs, out_specs=out_specs, check_vma=False
    )
```

time: 158 us -> 35.2 us (0.22)
  blocking collectives: 70.3 us -> 0 us
  waiting for transfers between devices: 36.8 us -> 0 us
  starting transfers between devices: 30.3 us -> 0 us
  Pallas kernels: 0 us -> 26.5 us
  matrix products: 6.05 us -> 0 us
  other arithmetic: 4.89 us -> 0 us
    all_gather x1 -> x0, blocking collectives: 70.3 us -> none  [per_device(): every_grad = lax.all_gather(dbag, ('group', 'dp'), axis=0, tiled=True)]
    all_to_all x8 -> x0, waiting for transfers between devices: 36.8 us -> none  [the longest x1 7.05 us: per_device(): lax.all_to_all(lax.all_to_all(partial_value.reshape(n_group, n_dp, CAP, w...]
    all_to_all x8 -> x0, starting transfers between devices: 30.3 us -> none  [the longest x1 6.24 us: per_device(): lax.all_to_all(lax.all_to_all(send_blk.reshape(n_group, n_dp, CAP), 'grou...]
    pallas_call x0 -> x1, Pallas kernels: none -> 26.5 us  [per_device(): pl.pallas_call(functools.partial(kernel, n_group, n_dp), out_shape=(jax.S...]
    unnamed x9 -> x16, local copies, waits for them, and re-layouts: 1.04 us -> 7.74 us
    dot_general x5 -> x0, matrix products: 6.05 us -> none  [the longest x1 1.57 us: per_device(): jnp.dot(place_b, pair_weight, preferred_element_type=jnp.float32)]
    all_to_all x8 -> x0, local copies, waits for them, and re-layouts: 3.07 us -> none  [the longest x1 0.76 us: per_device(): lax.all_to_all(partial_value.reshape(n_group, n_dp, CAP, width), 'group',...]
    reshape x6 -> x0, local copies, waits for them, and re-layouts: 2.33 us -> none  [the longest x2 0.79 us: per_device(): send_blk.reshape(n_group, n_dp, CAP)]
  transfers between devices with their start and end apart: 8 -> 0, of which waited for: 8 -> 0; matrix products, arithmetic and copies ran while one was open for 4% -> 0% of each run, Pallas kernels for 0% -> 0%
where the time goes in v1:
time: 35.2 us; the launch traced here: 34.9 us
  Pallas kernels  26.5 us (75%)
  local copies, waits for them, and re-layouts  7.74 us (22%)
  between operations  0.66 us (2%)
    pallas_call x1, Pallas kernels, per_device(): pl.pallas_call(functools.partial(kernel, n_group, n_dp), out_shape=(jax.S...  26.5 us
    unnamed x16, local copies, waits for them, and re-layouts  7.74 us

profile of v1, /device:TPU:0, one launch (start us, length us, event | category | flops | bytes accessed | tf_op | source)
XLA Modules:
  0.0 34.9 jit_solution(10171303997405140976)
XLA Ops:
  0.6 0.0 copy-start
  0.6 1.6 %copy-done = bf16[1024,1024]{1,0:T(8,128)(2,1)S(1)} copy-done((bf16[1024,1024]{1,0:T(8,128)(2,1)S(1)}, bf16[1024,1024]{1,0:T(8,128)(2,1)}, u32[]{:S(2)}) %copy-start) | copy-done | bytes 2097176
  2.2 0.0 copy-start.1
  2.2 1.2 %copy-done.1 = bf16[512,1024]{1,0:T(8,128)(2,1)S(1)} copy-done((bf16[512,1024]{1,0:T(8,128)(2,1)S(1)}, bf16[512,1024]{1,0:T(8,128)(2,1)}, u32[]{:S(2)}) %copy-start.1) | copy-done | bytes 1048600
  3.4 0.0 copy-start.2
  3.5 0.7 %copy-done.2 = bf16[32,128]{1,0:T(8,128)(2,1)S(1)} copy-done((bf16[32,128]{1,0:T(8,128)(2,1)S(1)}, bf16[32,128]{1,0:T(8,128)(2,1)}, u32[]{:S(2)}) %copy-start.2) | copy-done | bytes 8216
  4.1 0.0 copy-start.3
  4.1 0.7 %copy-done.3 = bf16[4,1024]{1,0:T(4,128)(2,1)S(1)} copy-done((bf16[4,1024]{1,0:T(4,128)(2,1)S(1)}, bf16[4,1024]{1,0:T(4,128)(2,1)}, u32[]{:S(2)}) %copy-start.3) | copy-done | bytes 8216
  4.8 0.0 copy-start.4
  4.8 0.7 %copy-done.4 = f32[512]{0:T(512)S(1)} copy-done((f32[512]{0:T(512)S(1)}, f32[512]{0:T(512)}, u32[]{:S(2)}) %copy-start.4) | copy-done | bytes 2072
  5.5 0.0 copy-start.5
  5.5 0.7 %copy-done.5 = s32[32]{0:T(128)S(1)} copy-done((s32[32]{0:T(128)S(1)}, s32[32]{0:T(128)}, u32[]{:S(2)}) %copy-start.5) | copy-done | bytes 152
  6.2 0.0 copy-start.6
  6.2 0.7 %copy-done.6 = s32[32]{0:T(128)S(1)} copy-done((s32[32]{0:T(128)S(1)}, s32[32]{0:T(128)}, u32[]{:S(2)}) %copy-start.6) | copy-done | bytes 152
  6.8 26.5 %bags.1 = (bf16[512,1024]{1,0:T(8,128)(2,1)S(1)}, f32[4,128]{1,0:T(4,128)S(1)}) custom-call(s32[1,32]{1,0:T(1,128)S(1)} %bitcast.6, s32[1,32]{1,0:T(1,128)S(1)} %bitcast.7, bf16[32,128]{1,0:T(8,128)(2,1)S(1)} %copy-done.2, bf16[4,1024]{1,0:T(4,128)(2,1)S(1)} %copy-done.3, f32[4,128]{1,0:T(4,128)S(1)} %bitcast.4, bf16[512,1024]{1,0:T(8,128)(2,1)S(1)} %copy-done.1, ...), custom_call_target="tpu_custom_call" | custom-call | tf_op jit(solution)/shard_map/bags/pallas_call | solution.py:288
  33.3 1.0 %copy.11 = bf16[512,1024]{1,0:T(8,128)(2,1)} copy(bf16[512,1024]{1,0:T(8,128)(2,1)S(1)} %get-tuple-element.8) | data formatting | bytes 2097152
  34.3 0.6 %copy.12 = f32[512]{0:T(512)} copy(f32[512]{0:T(512)S(1)} %bitcast.5) | data formatting | bytes 4096
Async XLA Ops:
  0.6 1.6 %copy-start = (bf16[1024,1024]{1,0:T(8,128)(2,1)S(1)}, bf16[1024,1024]{1,0:T(8,128)(2,1)}, u32[]{:S(2)}) copy-start(bf16[1024,1024]{1,0:T(8,128)(2,1)} %hid_hbm.1) | copy-start | bytes 6291460
  2.2 1.2 %copy-start.1 = (bf16[512,1024]{1,0:T(8,128)(2,1)S(1)}, bf16[512,1024]{1,0:T(8,128)(2,1)}, u32[]{:S(2)}) copy-start(bf16[512,1024]{1,0:T(8,128)(2,1)} %table_hbm.1) | copy-start | bytes 3145732
  3.4 0.7 %copy-start.2 = (bf16[32,128]{1,0:T(8,128)(2,1)S(1)}, bf16[32,128]{1,0:T(8,128)(2,1)}, u32[]{:S(2)}) copy-start(bf16[32,128]{1,0:T(8,128)(2,1)} %w_ref.1) | copy-start | bytes 24580
  4.1 0.7 %copy-start.3 = (bf16[4,1024]{1,0:T(4,128)(2,1)S(1)}, bf16[4,1024]{1,0:T(4,128)(2,1)}, u32[]{:S(2)}) copy-start(bf16[4,1024]{1,0:T(4,128)(2,1)} %cot_ref.1) | copy-start | bytes 24580
  4.8 0.7 %copy-start.4 = (f32[512]{0:T(512)S(1)}, f32[512]{0:T(512)}, u32[]{:S(2)}) copy-start(f32[512]{0:T(512)} %param.8) | copy-start | bytes 6148
  5.5 0.7 %copy-start.5 = (s32[32]{0:T(128)S(1)}, s32[32]{0:T(128)}, u32[]{:S(2)}) copy-start(s32[32]{0:T(128)} %param.9) | copy-start | bytes 388
  6.2 0.7 %copy-start.6 = (s32[32]{0:T(128)S(1)}, s32[32]{0:T(128)}, u32[]{:S(2)}) copy-start(s32[32]{0:T(128)} %param.10) | copy-start | bytes 388

commit v2 on v1

--- a/solution.py
+++ b/solution.py
@@ -11,6 +11,7 @@
 LANES = 128
 TOGETHER = 16
 PAD = 8
+LIMIT = 64 * 1024 * 1024
 MESH = pl.DeviceIdType.MESH
 BF = jnp.bfloat16
 F32 = jnp.float32
@@ -35,17 +36,23 @@
 def kernel(
     n_group,
     n_dp,
+    blk_hbm,
+    prot_hbm,
+    w_hbm,
+    cot_hbm,
+    accum_hbm,
+    table_hbm,
+    hid_hbm,
+    out_hbm,
+    acc_hbm,
     blk_ref,
     prot_ref,
     w_ref,
     cot_ref,
     accum_ref,
-    table_hbm,
-    hid_hbm,
-    out_hbm,
-    acc_ref,
     table,
     hid,
+    acc_ref,
     rows_out,
     send_w,
     got_w,
@@ -65,10 +72,15 @@
 ):
     n = n_group * n_dp
     me = lax.axis_index("group") * n_dp + lax.axis_index("dp")
-    load_table = pltpu.make_async_copy(table_hbm, table, loads.at[0])
-    load_hid = pltpu.make_async_copy(hid_hbm, hid, loads.at[1])
-    load_table.start()
-    load_hid.start()
+    pairs_of = [(blk_hbm, blk_ref), (prot_hbm, prot_ref), (w_hbm, w_ref)]
+    others_of = [(table_hbm, table), (hid_hbm, hid), (cot_hbm, cot_ref), (accum_hbm, accum_ref)]
+    copies = [
+        pltpu.make_async_copy(a, b, loads.at[i]) for i, (a, b) in enumerate(pairs_of + others_of)
+    ]
+    for copy in copies:
+        copy.start()
+    load_pairs = copies[:3]
+    load_table, load_hid, load_cot, load_accum = copies[3:]
 
     def where_is(t):
         return (lax.div(t, n_dp), lax.rem(t, n_dp))
@@ -129,6 +141,8 @@
     def at(g, size):
         return pl.ds(g * size, size) if few else pl.ds(pl.multiple_of(g * size, size), size)
 
+    for copy in load_pairs:
+        copy.wait()
     blk = blk_ref[...]
     owner = lax.div(blk, blocks)
     local = lax.rem(blk, blocks)
@@ -212,6 +226,7 @@
 
     dense_t[...] = dense[...].astype(F32).T.astype(BF)
     load_hid.wait()
+    load_accum.wait()
     arrived(got_part, 1)
 
     def bag_of(g):
@@ -224,6 +239,7 @@
             0, groups, lambda g, c: c + bag_of(g), jnp.zeros((chunks * PAD, LANES), F32)
         )
     bag = jnp.concatenate([stack[c * PAD : (c + 1) * PAD] for c in range(chunks)], axis=1)
+    load_cot.wait()
     cot = cot_ref[...].astype(F32)
     cot = jnp.concatenate([cot, jnp.zeros((PAD - proteins, cot.shape[1]), F32)], axis=0)
     inv = lax.rsqrt(jnp.mean(bag * bag, axis=-1, keepdims=True) + 1e-06)
@@ -266,6 +282,9 @@
         write.start()
         writes.append(write)
         acc_ref[b : b + 1, :] = jnp.sum(jnp.where(diagonal, new, 0.0), axis=0, keepdims=True)
+    write = pltpu.make_async_copy(acc_ref, acc_hbm, stores.at[blocks])
+    write.start()
+    writes.append(write)
     left(send_grad, 2)
     for write in writes:
         write.wait()
@@ -281,7 +300,6 @@
     tile = (width // LANES) * CAP
     slots = n * CAP
     step = min(TOGETHER, n)
-    vmem = pl.BlockSpec(memory_space=pltpu.VMEM)
     hbm = pl.BlockSpec(memory_space=pl.ANY)
     tiles = pltpu.VMEM((n, tile, LANES), BF)
     stack = (width // LANES) * PAD
@@ -291,11 +309,17 @@
             jax.ShapeDtypeStruct(table.shape, BF),
             jax.ShapeDtypeStruct((blocks, block_rows), F32),
         ),
-        in_specs=[vmem] * 5 + [hbm] * 2,
-        out_specs=(hbm, vmem),
+        in_specs=[hbm] * 7,
+        out_specs=(hbm, hbm),
         scratch_shapes=[
+            pltpu.VMEM((1, pairs), jnp.int32),
+            pltpu.VMEM((1, pairs), jnp.int32),
+            pltpu.VMEM(pair_weight.shape, BF),
+            pltpu.VMEM(hidden_cot.shape, BF),
+            pltpu.VMEM((blocks, block_rows), F32),
             pltpu.VMEM(table.shape, BF),
             pltpu.VMEM(w_hidden.shape, BF),
+            pltpu.VMEM((blocks, block_rows), F32),
             pltpu.VMEM(table.shape, BF),
             tiles,
             tiles,
@@ -310,11 +334,11 @@
             pltpu.VMEM((n * tile, stack), BF),
             pltpu.SemaphoreType.DMA((3,)),
             pltpu.SemaphoreType.DMA((3,)),
-            pltpu.SemaphoreType.DMA((2,)),
-            pltpu.SemaphoreType.DMA((blocks,)),
+            pltpu.SemaphoreType.DMA((7,)),
+            pltpu.SemaphoreType.DMA((blocks + 1,)),
         ],
         compiler_params=pltpu.CompilerParams(
-            collective_id=0, has_side_effects=True, vmem_limit_bytes=48 * 1024 * 1024
+            collective_id=0, has_side_effects=True, vmem_limit_bytes=LIMIT
         ),
         name="bags",
     )(

time: 35.2 us -> 30 us (0.85)
  local copies, waits for them, and re-layouts: 7.74 us -> 2.85 us
    unnamed x16 -> x4, local copies, waits for them, and re-layouts: 7.74 us -> 2.85 us
where the time goes in v2:
time: 30 us; the launch traced here: 29.8 us
  Pallas kernels  26.3 us (88%)
  local copies, waits for them, and re-layouts  2.85 us (10%)
  between operations  0.65 us (2%)
    pallas_call x1, Pallas kernels, per_device(): pl.pallas_call(functools.partial(kernel, n_group, n_dp), out_shape=(jax.S...  26.3 us
    unnamed x4, local copies, waits for them, and re-layouts  2.85 us

profile of v2, /device:TPU:0, one launch (start us, length us, event | category | flops | bytes accessed | tf_op | source)
XLA Modules:
  0.0 29.8 jit_solution(17296696791734962440)
XLA Ops:
  0.6 26.3 %bags.1 = (bf16[512,1024]{1,0:T(8,128)(2,1)}, f32[4,128]{1,0:T(4,128)}) custom-call(s32[1,32]{1,0:T(1,128)} %bitcast.6, s32[1,32]{1,0:T(1,128)} %bitcast.7, bf16[32,128]{1,0:T(8,128)(2,1)} %w_hbm.1, bf16[4,1024]{1,0:T(4,128)(2,1)} %cot_hbm.1, f32[4,128]{1,0:T(4,128)} %bitcast.4, bf16[512,1024]{1,0:T(8,128)(2,1)} %table_hbm.1, bf16[1024,1024]{1,0:T(8,128)(2,1)} %hid_hbm.1), custom_call_target="tpu_custom_call" | custom-call | tf_op jit(solution)/shard_map/bags/pallas_call | solution.py:306
  26.9 0.0 copy-start
  26.9 2.3 %copy.11 = bf16[512,1024]{1,0:T(8,128)(2,1)} copy(bf16[512,1024]{1,0:T(8,128)(2,1)} %get-tuple-element.8) | data formatting | bytes 2097152
  29.2 0.0 copy-done
  29.2 0.6 %copy.12 = f32[512]{0:T(512)} copy(f32[512]{0:T(512)S(1)} %bitcast.5) | data formatting | bytes 4096
Async XLA Ops:
  26.9 2.3 %copy-start = (f32[4,128]{1,0:T(4,128)S(1)}, f32[4,128]{1,0:T(4,128)}, u32[]{:S(2)}) copy-start(f32[4,128]{1,0:T(4,128)} %get-tuple-element.5) | copy-start | bytes 6148

commit v3 on v2

--- a/solution.py
+++ b/solution.py
@@ -33,6 +33,26 @@
     return jnp.where(mask, 1.0, 0.0).astype(BF)
 
 
+def repack(step, chunks):
+    tile, stacked = chunks * CAP, step * CAP
+    shape = (step * tile, step * tile)
+    to_r, to_c = iota(shape, 0), iota(shape, 1)
+    r_c, r_d, r_k = to_r // stacked, (to_r % stacked) // CAP, to_r % CAP
+    unpack = ones_where(to_c == r_d * tile + r_c * CAP + r_k)
+    t_c, t_d, t_k = to_c // stacked, (to_c % stacked) // CAP, to_c % CAP
+    pack = ones_where(to_r == t_d * tile + t_c * CAP + t_k)
+    return pack, unpack
+
+
+def unpacked(unpack, tiles, count):
+    step, tile, lanes = tiles.shape
+    stacked = step * CAP
+    high = dot(unpack[: count * stacked], tiles.reshape(step * tile, lanes))
+    return jnp.concatenate(
+        [high[c * stacked : (c + 1) * stacked] for c in range(count)], axis=1
+    ).astype(BF)
+
+
 def kernel(
     n_group,
     n_dp,
@@ -40,29 +60,23 @@
     prot_hbm,
     w_hbm,
     cot_hbm,
-    accum_hbm,
     table_hbm,
     hid_hbm,
-    out_hbm,
-    acc_hbm,
+    got_grad,
+    dense_t_hbm,
     blk_ref,
     prot_ref,
     w_ref,
     cot_ref,
-    accum_ref,
     table,
     hid,
-    acc_ref,
-    rows_out,
     send_w,
     got_w,
     send_part,
     got_part,
     send_grad,
-    got_grad,
     dense,
     dense_t,
-    gathered,
     pick,
     pick_t,
     sends,
@@ -73,14 +87,14 @@
     n = n_group * n_dp
     me = lax.axis_index("group") * n_dp + lax.axis_index("dp")
     pairs_of = [(blk_hbm, blk_ref), (prot_hbm, prot_ref), (w_hbm, w_ref)]
-    others_of = [(table_hbm, table), (hid_hbm, hid), (cot_hbm, cot_ref), (accum_hbm, accum_ref)]
+    others_of = [(table_hbm, table), (hid_hbm, hid), (cot_hbm, cot_ref)]
     copies = [
         pltpu.make_async_copy(a, b, loads.at[i]) for i, (a, b) in enumerate(pairs_of + others_of)
     ]
     for copy in copies:
         copy.start()
     load_pairs = copies[:3]
-    load_table, load_hid, load_cot, load_accum = copies[3:]
+    load_table, load_hid, load_cot = copies[3:]
 
     def where_is(t):
         return (lax.div(t, n_dp), lax.rem(t, n_dp))
@@ -108,7 +122,6 @@
             return carry
 
         lax.fori_loop(1, n, start, 0)
-        got[me] = send[me]
 
     others = pl.ds(0, n - 1)
 
@@ -173,6 +186,7 @@
     each(make_w)
     pl.semaphore_wait(barrier, n - 1)
     exchange(send_w, got_w, 0)
+    got_w[me] = send_w[me]
 
     def make_pick(g):
         place = ones_where(place_of(g))
@@ -181,24 +195,12 @@
 
     each(make_pick)
 
-    to_r, to_c = iota((rows, rows), 0), iota((rows, rows), 1)
     stacked = step * CAP
-    r_c, r_d, r_k = to_r // stacked, (to_r % stacked) // CAP, to_r % CAP
-    unpack = ones_where(to_c == r_d * tile + r_c * CAP + r_k)
-    t_c, t_d, t_k = to_c // stacked, (to_c % stacked) // CAP, to_c % CAP
-    pack = ones_where(to_r == t_d * tile + t_c * CAP + t_k)
-
-    def unpacked(got, g, count):
-        flat = got[at(g, step)].reshape(rows, LANES)
-        high = dot(unpack[: count * stacked], flat)
-        return jnp.concatenate(
-            [high[c * stacked : (c + 1) * stacked] for c in range(count)], axis=1
-        )
-
+    pack, unpack = repack(step, chunks)
     arrived(got_w, 0)
 
     def make_dense(g):
-        dense[at(g, stacked), :] = unpacked(got_w, g, blocks * block_rows // LANES).astype(BF)
+        dense[at(g, stacked), :] = unpacked(unpack, got_w[at(g, step)], blocks * block_rows // LANES)
 
     each(make_dense)
     load_table.wait()
@@ -223,10 +225,12 @@
     else:
         lax.fori_loop(0, slots // big, lambda h, c: (make_part(h), c)[1], 0)
     exchange(send_part, got_part, 1)
+    got_part[me] = send_part[me]
 
     dense_t[...] = dense[...].astype(F32).T.astype(BF)
+    store_dense = pltpu.make_async_copy(dense_t, dense_t_hbm, stores.at[0])
+    store_dense.start()
     load_hid.wait()
-    load_accum.wait()
     arrived(got_part, 1)
 
     def bag_of(g):
@@ -260,32 +264,78 @@
 
     each(make_grad)
     exchange(send_grad, got_grad, 2)
+    own = pltpu.make_async_copy(send_grad.at[me], got_grad.at[me], stores.at[1])
+    own.start()
     left(send_w, 0)
     left(send_part, 1)
+    left(send_grad, 2)
+    store_dense.wait()
+    own.wait()
     arrived(got_grad, 2)
 
+
+def update(
+    dense_hbm,
+    tiles_hbm,
+    accum_hbm,
+    table_hbm,
+    out_hbm,
+    acc_hbm,
+    dense_t,
+    tiles,
+    accum,
+    table,
+    rows_out,
+    acc_out,
+    gathered,
+    loads,
+    stores,
+):
+    n, tile, _ = tiles.shape
+    blocks, block_rows = accum.shape
+    chunks = tile // CAP
+    step = min(TOGETHER, n)
+    groups = n // step
+    stacked = step * CAP
+    parts = [pl.ds(b * block_rows, block_rows) for b in range(blocks)]
+    pairs_of = [(tiles_hbm, tiles), (dense_hbm, dense_t), (accum_hbm, accum)]
+    pairs_of += [(table_hbm.at[some], table.at[some]) for some in parts]
+    copies = [pltpu.make_async_copy(a, b, loads.at[i]) for i, (a, b) in enumerate(pairs_of)]
+    for copy in copies:
+        copy.start()
+    _, unpack = repack(step, chunks)
+    diagonal = iota((block_rows, block_rows), 0) == iota((block_rows, block_rows), 1)
+    copies[0].wait()
+
     def make_gathered(g):
-        gathered[at(g, stacked), :] = unpacked(got_grad, g, chunks).astype(BF)
-
-    each(make_gathered)
-    diagonal = iota((block_rows, block_rows), 0) == iota((block_rows, block_rows), 1)
+        few = groups <= 4
+        gathered[pl.ds(g * stacked if few else pl.multiple_of(g * stacked, stacked), stacked), :] = (
+            unpacked(unpack, tiles[pl.ds(g * step, step)], chunks)
+        )
+
+    if groups <= 4:
+        for g in range(groups):
+            make_gathered(g)
+    else:
+        lax.fori_loop(0, groups, lambda g, c: (make_gathered(g), c)[1], 0)
+    copies[1].wait()
+    copies[2].wait()
     writes = []
-    for b in range(blocks):
-        some = pl.ds(b * block_rows, block_rows)
+    for b, some in enumerate(parts):
         grad = dot(dense_t[some, :], gathered[...])
         mean = jnp.mean(grad * grad, axis=-1, keepdims=True)
-        old = jnp.sum(jnp.where(diagonal, accum_ref[b : b + 1, :], 0.0), axis=1, keepdims=True)
+        old = jnp.sum(jnp.where(diagonal, accum[b : b + 1, :], 0.0), axis=1, keepdims=True)
         new = old + mean
         scale = 0.3 / (jnp.sqrt(new) + 1e-08)
+        copies[3 + b].wait()
         rows_out[some, :] = (table[some, :].astype(F32) - grad * scale).astype(BF)
         write = pltpu.make_async_copy(rows_out.at[some], out_hbm.at[some], stores.at[b])
         write.start()
         writes.append(write)
-        acc_ref[b : b + 1, :] = jnp.sum(jnp.where(diagonal, new, 0.0), axis=0, keepdims=True)
-    write = pltpu.make_async_copy(acc_ref, acc_hbm, stores.at[blocks])
+        acc_out[b : b + 1, :] = jnp.sum(jnp.where(diagonal, new, 0.0), axis=0, keepdims=True)
+    write = pltpu.make_async_copy(acc_out, acc_hbm, stores.at[blocks])
     write.start()
     writes.append(write)
-    left(send_grad, 2)
     for write in writes:
         write.wait()
 
@@ -303,25 +353,21 @@
     hbm = pl.BlockSpec(memory_space=pl.ANY)
     tiles = pltpu.VMEM((n, tile, LANES), BF)
     stack = (width // LANES) * PAD
-    new_table, new_accum = pl.pallas_call(
+    got_grad, dense_t = pl.pallas_call(
         functools.partial(kernel, n_group, n_dp),
         out_shape=(
-            jax.ShapeDtypeStruct(table.shape, BF),
-            jax.ShapeDtypeStruct((blocks, block_rows), F32),
+            jax.ShapeDtypeStruct((n, tile, LANES), BF),
+            jax.ShapeDtypeStruct((rows_dev, slots), BF),
         ),
-        in_specs=[hbm] * 7,
+        in_specs=[hbm] * 6,
         out_specs=(hbm, hbm),
         scratch_shapes=[
             pltpu.VMEM((1, pairs), jnp.int32),
             pltpu.VMEM((1, pairs), jnp.int32),
             pltpu.VMEM(pair_weight.shape, BF),
             pltpu.VMEM(hidden_cot.shape, BF),
-            pltpu.VMEM((blocks, block_rows), F32),
             pltpu.VMEM(table.shape, BF),
             pltpu.VMEM(w_hidden.shape, BF),
-            pltpu.VMEM((blocks, block_rows), F32),
-            pltpu.VMEM(table.shape, BF),
-            tiles,
             tiles,
             tiles,
             tiles,
@@ -329,13 +375,12 @@
             tiles,
             pltpu.VMEM((slots, rows_dev), BF),
             pltpu.VMEM((rows_dev, slots), BF),
-            pltpu.VMEM((slots, width), BF),
             pltpu.VMEM((n // step, stack, step * tile), BF),
             pltpu.VMEM((n * tile, stack), BF),
             pltpu.SemaphoreType.DMA((3,)),
             pltpu.SemaphoreType.DMA((3,)),
-            pltpu.SemaphoreType.DMA((7,)),
-            pltpu.SemaphoreType.DMA((blocks + 1,)),
+            pltpu.SemaphoreType.DMA((6,)),
+            pltpu.SemaphoreType.DMA((2,)),
         ],
         compiler_params=pltpu.CompilerParams(
             collective_id=0, has_side_effects=True, vmem_limit_bytes=LIMIT
@@ -346,10 +391,31 @@
         pair_protein.reshape(1, pairs),
         pair_weight,
         hidden_cot,
-        accum.reshape(blocks, block_rows),
         table,
         w_hidden,
     )
+    new_table, new_accum = pl.pallas_call(
+        update,
+        out_shape=(
+            jax.ShapeDtypeStruct(table.shape, BF),
+            jax.ShapeDtypeStruct((blocks, block_rows), F32),
+        ),
+        in_specs=[hbm] * 4,
+        out_specs=(hbm, hbm),
+        scratch_shapes=[
+            pltpu.VMEM((rows_dev, slots), BF),
+            tiles,
+            pltpu.VMEM((blocks, block_rows), F32),
+            pltpu.VMEM(table.shape, BF),
+            pltpu.VMEM(table.shape, BF),
+            pltpu.VMEM((blocks, block_rows), F32),
+            pltpu.VMEM((slots, width), BF),
+            pltpu.SemaphoreType.DMA((3 + blocks,)),
+            pltpu.SemaphoreType.DMA((1 + blocks,)),
+        ],
+        compiler_params=pltpu.CompilerParams(vmem_limit_bytes=LIMIT),
+        name="update",
+    )(dense_t, got_grad, accum.reshape(blocks, block_rows), table)
     return new_table, new_accum.reshape(rows_dev)
 
 

time: 30 us -> 29 us (0.967)
  local copies, waits for them, and re-layouts: 2.85 us -> 0 us
  Pallas kernels: 26.3 us -> 28.2 us
    pallas_call x0 -> x1, Pallas kernels: none -> 3.39 us  [per_device(): pl.pallas_call(update, out_shape=(jax.ShapeDtypeStruct(table.shape, BF),...]
    unnamed x4 -> x0, local copies, waits for them, and re-layouts: 2.85 us -> none
    pallas_call x1, Pallas kernels: 26.3 us -> 24.8 us  [per_device(): pl.pallas_call(functools.partial(kernel, n_group, n_dp), out_shape=(jax.S...]
where the time goes in v3:
time: 29 us; the launch traced here: 28.8 us
  Pallas kernels  28.2 us (97%)
  between operations  0.64 us (2%)
    pallas_call x1, Pallas kernels, per_device(): pl.pallas_call(functools.partial(kernel, n_group, n_dp), out_shape=(jax.S...  24.8 us
    pallas_call x1, Pallas kernels, per_device(): pl.pallas_call(update, out_shape=(jax.ShapeDtypeStruct(table.shape, BF),...  3.39 us

profile of v3, /device:TPU:0, one launch (start us, length us, event | category | flops | bytes accessed | tf_op | source)
XLA Modules:
  0.0 28.8 jit_solution(7867246246539663010)
XLA Ops:
  0.6 24.8 %bags.1 = (bf16[32,16,128]{2,1,0:T(8,128)(2,1)}, bf16[512,64]{1,0:T(8,128)(2,1)}) custom-call(s32[1,32]{1,0:T(1,128)} %bitcast.5, s32[1,32]{1,0:T(1,128)} %bitcast.6, bf16[32,128]{1,0:T(8,128)(2,1)} %w_hbm.1, bf16[4,1024]{1,0:T(4,128)(2,1)} %cot_hbm.1, bf16[512,1024]{1,0:T(8,128)(2,1)} %table_hbm.3, bf16[1024,1024]{1,0:T(8,128)(2,1)} %hid_hbm.1), custom_call_target="tpu_custom_call" | custom-call | tf_op jit(solution)/shard_map/bags/pallas_call | solution.py:356
  25.4 3.4 %update.1 = (bf16[512,1024]{1,0:T(8,128)(2,1)}, f32[4,128]{1,0:T(4,128)}) custom-call(bf16[512,64]{1,0:T(8,128)(2,1)} %get-tuple-element.6.dense_hbm, bf16[32,16,128]{2,1,0:T(8,128)(2,1)} %get-tuple-element.7.tiles_hbm, f32[4,128]{1,0:T(4,128)} %bitcast.4, bf16[512,1024]{1,0:T(8,128)(2,1)} %table_hbm.3), custom_call_target="tpu_custom_call" | custom-call | tf_op jit(solution)/shard_map/update/pallas_call | solution.py:397

commit v4 on v3

--- a/solution.py
+++ b/solution.py
@@ -11,7 +11,7 @@
 LANES = 128
 TOGETHER = 16
 PAD = 8
-LIMIT = 64 * 1024 * 1024
+LIMIT = 40 * 1024 * 1024
 MESH = pl.DeviceIdType.MESH
 BF = jnp.bfloat16
 F32 = jnp.float32
@@ -60,15 +60,17 @@
     prot_hbm,
     w_hbm,
     cot_hbm,
+    accum_hbm,
     table_hbm,
     hid_hbm,
     got_grad,
-    dense_t_hbm,
+    dense_t,
+    accum,
+    table,
     blk_ref,
     prot_ref,
     w_ref,
     cot_ref,
-    table,
     hid,
     send_w,
     got_w,
@@ -76,52 +78,61 @@
     got_part,
     send_grad,
     dense,
-    dense_t,
     pick,
     pick_t,
     sends,
     recvs,
     loads,
-    stores,
 ):
     n = n_group * n_dp
-    me = lax.axis_index("group") * n_dp + lax.axis_index("dp")
+    mine = (lax.axis_index("group"), lax.axis_index("dp"))
+    me = mine[0] * n_dp + mine[1]
     pairs_of = [(blk_hbm, blk_ref), (prot_hbm, prot_ref), (w_hbm, w_ref)]
-    others_of = [(table_hbm, table), (hid_hbm, hid), (cot_hbm, cot_ref)]
+    others_of = [(table_hbm, table), (hid_hbm, hid), (cot_hbm, cot_ref), (accum_hbm, accum)]
     copies = [
         pltpu.make_async_copy(a, b, loads.at[i]) for i, (a, b) in enumerate(pairs_of + others_of)
     ]
     for copy in copies:
         copy.start()
     load_pairs = copies[:3]
-    load_table, load_hid, load_cot = copies[3:]
-
-    def where_is(t):
-        return (lax.div(t, n_dp), lax.rem(t, n_dp))
+    load_table, load_hid, load_cot, load_accum = copies[3:]
+
+    def to_all(act):
+        if n <= 32:
+            at_group = [lax.rem(mine[0] + a, n_group) for a in range(n_group)]
+            at_dp = [lax.rem(mine[1] + b, n_dp) for b in range(n_dp)]
+            for b in sorted(range(n_dp), key=lambda b: -min(b, n_dp - b)):
+                for a in range(n_group):
+                    if a or b:
+                        act((at_group[a], at_dp[b]), at_group[a] * n_dp + at_dp[b])
+        else:
+
+            def one(i, carry):
+                t = lax.rem(me + i, n)
+                act((lax.div(t, n_dp), lax.rem(t, n_dp)), t)
+                return carry
+
+            lax.fori_loop(1, n, one, 0)
 
     barrier = pltpu.get_barrier_semaphore()
-
-    def greet(i, carry):
-        t = lax.rem(me + i, n)
-        pl.semaphore_signal(barrier, inc=1, device_id=where_is(t), device_id_type=MESH)
-        return carry
-
-    lax.fori_loop(1, n, greet, 0)
+    to_all(
+        lambda device, t: pl.semaphore_signal(
+            barrier, inc=1, device_id=device, device_id_type=MESH
+        )
+    )
 
     def exchange(send, got, phase):
-        def start(i, carry):
-            t = lax.rem(me + i, n)
-            pltpu.make_async_remote_copy(
+        to_all(
+            lambda device, t: pltpu.make_async_remote_copy(
                 src_ref=send.at[t],
                 dst_ref=got.at[me],
                 send_sem=sends.at[phase],
                 recv_sem=recvs.at[phase],
-                device_id=where_is(t),
+                device_id=device,
                 device_id_type=MESH,
             ).start()
-            return carry
-
-        lax.fori_loop(1, n, start, 0)
+        )
+        got[me] = send[me]
 
     others = pl.ds(0, n - 1)
 
@@ -186,7 +197,6 @@
     each(make_w)
     pl.semaphore_wait(barrier, n - 1)
     exchange(send_w, got_w, 0)
-    got_w[me] = send_w[me]
 
     def make_pick(g):
         place = ones_where(place_of(g))
@@ -225,11 +235,9 @@
     else:
         lax.fori_loop(0, slots // big, lambda h, c: (make_part(h), c)[1], 0)
     exchange(send_part, got_part, 1)
-    got_part[me] = send_part[me]
 
     dense_t[...] = dense[...].astype(F32).T.astype(BF)
-    store_dense = pltpu.make_async_copy(dense_t, dense_t_hbm, stores.at[0])
-    store_dense.start()
+    load_accum.wait()
     load_hid.wait()
     arrived(got_part, 1)
 
@@ -264,33 +272,13 @@
 
     each(make_grad)
     exchange(send_grad, got_grad, 2)
-    own = pltpu.make_async_copy(send_grad.at[me], got_grad.at[me], stores.at[1])
-    own.start()
     left(send_w, 0)
     left(send_part, 1)
     left(send_grad, 2)
-    store_dense.wait()
-    own.wait()
     arrived(got_grad, 2)
 
 
-def update(
-    dense_hbm,
-    tiles_hbm,
-    accum_hbm,
-    table_hbm,
-    out_hbm,
-    acc_hbm,
-    dense_t,
-    tiles,
-    accum,
-    table,
-    rows_out,
-    acc_out,
-    gathered,
-    loads,
-    stores,
-):
+def update(dense_t, tiles, accum, table, out_hbm, acc_hbm, rows_out, acc_out, gathered, stores):
     n, tile, _ = tiles.shape
     blocks, block_rows = accum.shape
     chunks = tile // CAP
@@ -298,14 +286,8 @@
     groups = n // step
     stacked = step * CAP
     parts = [pl.ds(b * block_rows, block_rows) for b in range(blocks)]
-    pairs_of = [(tiles_hbm, tiles), (dense_hbm, dense_t), (accum_hbm, accum)]
-    pairs_of += [(table_hbm.at[some], table.at[some]) for some in parts]
-    copies = [pltpu.make_async_copy(a, b, loads.at[i]) for i, (a, b) in enumerate(pairs_of)]
-    for copy in copies:
-        copy.start()
     _, unpack = repack(step, chunks)
     diagonal = iota((block_rows, block_rows), 0) == iota((block_rows, block_rows), 1)
-    copies[0].wait()
 
     def make_gathered(g):
         few = groups <= 4
@@ -318,8 +300,6 @@
             make_gathered(g)
     else:
         lax.fori_loop(0, groups, lambda g, c: (make_gathered(g), c)[1], 0)
-    copies[1].wait()
-    copies[2].wait()
     writes = []
     for b, some in enumerate(parts):
         grad = dot(dense_t[some, :], gathered[...])
@@ -327,7 +307,6 @@
         old = jnp.sum(jnp.where(diagonal, accum[b : b + 1, :], 0.0), axis=1, keepdims=True)
         new = old + mean
         scale = 0.3 / (jnp.sqrt(new) + 1e-08)
-        copies[3 + b].wait()
         rows_out[some, :] = (table[some, :].astype(F32) - grad * scale).astype(BF)
         write = pltpu.make_async_copy(rows_out.at[some], out_hbm.at[some], stores.at[b])
         write.start()
@@ -350,23 +329,25 @@
     tile = (width // LANES) * CAP
     slots = n * CAP
     step = min(TOGETHER, n)
-    hbm = pl.BlockSpec(memory_space=pl.ANY)
+    hbm = pl.BlockSpec(memory_space=pltpu.HBM)
+    vmem = pl.BlockSpec(memory_space=pltpu.VMEM)
     tiles = pltpu.VMEM((n, tile, LANES), BF)
     stack = (width // LANES) * PAD
-    got_grad, dense_t = pl.pallas_call(
+    got_grad, dense_t, accum_held, table_held = pl.pallas_call(
         functools.partial(kernel, n_group, n_dp),
         out_shape=(
             jax.ShapeDtypeStruct((n, tile, LANES), BF),
             jax.ShapeDtypeStruct((rows_dev, slots), BF),
+            jax.ShapeDtypeStruct((blocks, block_rows), F32),
+            jax.ShapeDtypeStruct(table.shape, BF),
         ),
-        in_specs=[hbm] * 6,
-        out_specs=(hbm, hbm),
+        in_specs=[hbm] * 7,
+        out_specs=(vmem,) * 4,
         scratch_shapes=[
             pltpu.VMEM((1, pairs), jnp.int32),
             pltpu.VMEM((1, pairs), jnp.int32),
             pltpu.VMEM(pair_weight.shape, BF),
             pltpu.VMEM(hidden_cot.shape, BF),
-            pltpu.VMEM(table.shape, BF),
             pltpu.VMEM(w_hidden.shape, BF),
             tiles,
             tiles,
@@ -374,25 +355,29 @@
             tiles,
             tiles,
             pltpu.VMEM((slots, rows_dev), BF),
-            pltpu.VMEM((rows_dev, slots), BF),
             pltpu.VMEM((n // step, stack, step * tile), BF),
             pltpu.VMEM((n * tile, stack), BF),
             pltpu.SemaphoreType.DMA((3,)),
             pltpu.SemaphoreType.DMA((3,)),
-            pltpu.SemaphoreType.DMA((6,)),
-            pltpu.SemaphoreType.DMA((2,)),
+            pltpu.SemaphoreType.DMA((7,)),
         ],
         compiler_params=pltpu.CompilerParams(
             collective_id=0, has_side_effects=True, vmem_limit_bytes=LIMIT
         ),
         name="bags",
     )(
-        pair_block.reshape(1, pairs),
-        pair_protein.reshape(1, pairs),
-        pair_weight,
-        hidden_cot,
-        table,
-        w_hidden,
+        *(
+            pltpu.with_memory_space_constraint(x, pltpu.HBM)
+            for x in (
+                pair_block.reshape(1, pairs),
+                pair_protein.reshape(1, pairs),
+                pair_weight,
+                hidden_cot,
+                accum.reshape(blocks, block_rows),
+                table,
+                w_hidden,
+            )
+        )
     )
     new_table, new_accum = pl.pallas_call(
         update,
@@ -400,22 +385,17 @@
             jax.ShapeDtypeStruct(table.shape, BF),
             jax.ShapeDtypeStruct((blocks, block_rows), F32),
         ),
-        in_specs=[hbm] * 4,
+        in_specs=[vmem] * 4,
         out_specs=(hbm, hbm),
         scratch_shapes=[
-            pltpu.VMEM((rows_dev, slots), BF),
-            tiles,
-            pltpu.VMEM((blocks, block_rows), F32),
-            pltpu.VMEM(table.shape, BF),
             pltpu.VMEM(table.shape, BF),
             pltpu.VMEM((blocks, block_rows), F32),
             pltpu.VMEM((slots, width), BF),
-            pltpu.SemaphoreType.DMA((3 + blocks,)),
             pltpu.SemaphoreType.DMA((1 + blocks,)),
         ],
-        compiler_params=pltpu.CompilerParams(vmem_limit_bytes=LIMIT),
+        compiler_params=pltpu.CompilerParams(vmem_limit_bytes=LIMIT // 2),
         name="update",
-    )(dense_t, got_grad, accum.reshape(blocks, block_rows), table)
+    )(dense_t, got_grad, accum_held, table_held)
     return new_table, new_accum.reshape(rows_dev)
 
 

time: 29 us -> 27.6 us (0.952)
  Pallas kernels: 28.2 us -> 26.8 us
    pallas_call x1, Pallas kernels: 3.39 us -> 1.68 us  [per_device(): pl.pallas_call(update, out_shape=(jax.ShapeDtypeStruct(table.shape, BF),...]
    pallas_call x1, Pallas kernels: 24.8 us -> 25.1 us  [per_device(): pl.pallas_call(functools.partial(kernel, n_group, n_dp), out_shape=(jax.S...]
where the time goes in v4:
time: 27.6 us; the launch traced here: 27.4 us
  Pallas kernels  26.8 us (97%)
  between operations  0.64 us (2%)
    pallas_call x1, Pallas kernels, per_device(): pl.pallas_call(functools.partial(kernel, n_group, n_dp), out_shape=(jax.S...  25.1 us
    pallas_call x1, Pallas kernels, per_device(): pl.pallas_call(update, out_shape=(jax.ShapeDtypeStruct(table.shape, BF),...  1.68 us

profile of v4, /device:TPU:0, one launch (start us, length us, event | category | flops | bytes accessed | tf_op | source)
XLA Modules:
  0.0 27.4 jit_solution(15432831724149682025)
XLA Ops:
  0.6 25.1 %bags.1 = (bf16[32,16,128]{2,1,0:T(8,128)(2,1)S(1)}, bf16[512,64]{1,0:T(8,128)(2,1)S(1)}, f32[4,128]{1,0:T(4,128)S(1)}, bf16[512,1024]{1,0:T(8,128)(2,1)S(1)}) custom-call(s32[1,32]{1,0:T(1,128)} %bitcast.5, s32[1,32]{1,0:T(1,128)} %bitcast.6, bf16[32,128]{1,0:T(8,128)(2,1)} %w_hbm.1, bf16[4,1024]{1,0:T(4,128)(2,1)} %cot_hbm.1, f32[4,128]{1,0:T(4,128)} %bitcast.4, ...), custom_call_target="tpu_custom_call" | custom-call | tf_op jit(solution)/shard_map/bags/pallas_call | solution.py:336
  25.8 1.7 %update.1 = (bf16[512,1024]{1,0:T(8,128)(2,1)}, f32[4,128]{1,0:T(4,128)}) custom-call(bf16[512,64]{1,0:T(8,128)(2,1)S(1)} %get-tuple-element.8.dense_t, bf16[32,16,128]{2,1,0:T(8,128)(2,1)S(1)} %get-tuple-element.9.tiles, f32[4,128]{1,0:T(4,128)S(1)} %get-tuple-element.10.accum, bf16[512,1024]{1,0:T(8,128)(2,1)S(1)} %get-tuple-element.11.table), custom_call_target="tpu_custom_call" | custom-call | tf_op jit(solution)/shard_map/update/pallas_call | solution.py:382

commit v5 on v4

--- a/solution.py
+++ b/solution.py
@@ -11,6 +11,7 @@
 LANES = 128
 TOGETHER = 16
 PAD = 8
+MARK = 2.0**-15
 LIMIT = 40 * 1024 * 1024
 MESH = pl.DeviceIdType.MESH
 BF = jnp.bfloat16
@@ -29,6 +30,14 @@
     return lax.broadcasted_iota(jnp.int32, shape, dim)
 
 
+def over(x, k):
+    return jnp.right_shift(x, k.bit_length() - 1)
+
+
+def rest(x, k):
+    return jnp.bitwise_and(x, k - 1)
+
+
 def ones_where(mask):
     return jnp.where(mask, 1.0, 0.0).astype(BF)
 
@@ -37,9 +46,9 @@
     tile, stacked = chunks * CAP, step * CAP
     shape = (step * tile, step * tile)
     to_r, to_c = iota(shape, 0), iota(shape, 1)
-    r_c, r_d, r_k = to_r // stacked, (to_r % stacked) // CAP, to_r % CAP
+    r_c, r_d, r_k = over(to_r, stacked), over(rest(to_r, stacked), CAP), rest(to_r, CAP)
     unpack = ones_where(to_c == r_d * tile + r_c * CAP + r_k)
-    t_c, t_d, t_k = to_c // stacked, (to_c % stacked) // CAP, to_c % CAP
+    t_c, t_d, t_k = over(to_c, stacked), over(rest(to_c, stacked), CAP), rest(to_c, CAP)
     pack = ones_where(to_r == t_d * tile + t_c * CAP + t_k)
     return pack, unpack
 
@@ -168,8 +177,8 @@
     for copy in load_pairs:
         copy.wait()
     blk = blk_ref[...]
-    owner = lax.div(blk, blocks)
-    local = lax.rem(blk, blocks)
+    owner = over(blk, blocks)
+    local = rest(blk, blocks)
     local_prot = prot_ref[...] - me * proteins
     square = (pairs, pairs)
     from_row, from_col = iota(square, 0), iota(square, 1)
@@ -180,23 +189,29 @@
     slot = owner * CAP + rank.astype(jnp.int32)
 
     place_rows = iota((rows, pairs), 0)
-    place_c = lax.rem(place_rows, tile) // CAP
-    place_slot = (place_rows // tile) * CAP + lax.rem(place_rows, CAP)
-    for_prot = ones_where(iota((chunks * PAD, pairs), 0) % PAD == local_prot)
-    same_c = iota((chunks * PAD, rows), 0) // PAD == (iota((chunks * PAD, rows), 1) % tile) // CAP
-    same_c_t = iota((rows, chunks * PAD), 1) // PAD == (iota((rows, chunks * PAD), 0) % tile) // CAP
+    place_slot = over(place_rows, tile) * CAP + rest(place_rows, CAP)
     weights = w_ref[...]
 
     def place_of(g):
         return place_slot + g * (step * CAP) == slot
 
+    slot_rows = iota((step * CAP, pairs), 0)
+
     def make_w(g):
-        place = place_of(g) & (place_c == local)
-        send_w[at(g, step)] = dot(ones_where(place), weights).astype(BF).reshape(step, tile, LANES)
+        place = slot_rows + g * (step * CAP) == slot
+        block = jnp.sum(jnp.where(place, local.astype(F32), 0.0), axis=1, keepdims=True)
+        marked = dot(ones_where(place), weights) * (1.0 + block * MARK)
+        send_w[at(g, step)] = marked.reshape(step, CAP, block_rows)
 
     each(make_w)
     pl.semaphore_wait(barrier, n - 1)
     exchange(send_w, got_w, 0)
+
+    for_prot = ones_where(rest(iota((chunks * PAD, pairs), 0), PAD) == local_prot)
+    shape = (chunks * PAD, rows)
+    same_c = over(iota(shape, 0), PAD) == over(rest(iota(shape, 1), tile), CAP)
+    shape = (rows, chunks * PAD)
+    same_c_t = over(iota(shape, 1), PAD) == over(rest(iota(shape, 0), tile), CAP)
 
     def make_pick(g):
         place = ones_where(place_of(g))
@@ -206,11 +221,16 @@
     each(make_pick)
 
     stacked = step * CAP
-    pack, unpack = repack(step, chunks)
+    pack, _ = repack(step, chunks)
     arrived(got_w, 0)
 
     def make_dense(g):
-        dense[at(g, stacked), :] = unpacked(unpack, got_w[at(g, step)], blocks * block_rows // LANES)
+        marked = got_w[at(g, step)].reshape(stacked, block_rows)
+        plain = marked.astype(BF).astype(F32)
+        dense[at(g, stacked), :] = jnp.concatenate(
+            [jnp.where(marked == plain * (1.0 + b * MARK), plain, 0.0) for b in range(blocks)],
+            axis=1,
+        ).astype(BF)
 
     each(make_dense)
     load_table.wait()
@@ -349,8 +369,8 @@
             pltpu.VMEM(pair_weight.shape, BF),
             pltpu.VMEM(hidden_cot.shape, BF),
             pltpu.VMEM(w_hidden.shape, BF),
-            tiles,
-            tiles,
+            pltpu.VMEM((n, CAP, block_rows), F32),
+            pltpu.VMEM((n, CAP, block_rows), F32),
             tiles,
             tiles,
             tiles,

time: 27.6 us -> 26.3 us (0.953)
  Pallas kernels: 26.8 us -> 25.5 us
    pallas_call x1, Pallas kernels: 25.1 us -> 23.8 us  [per_device(): pl.pallas_call(functools.partial(kernel, n_group, n_dp), out_shape=(jax.S...]
where the time goes in v5:
time: 26.3 us; the launch traced here: 26.1 us
  Pallas kernels  25.5 us (97%)
  between operations  0.64 us (2%)
    pallas_call x1, Pallas kernels, per_device(): pl.pallas_call(functools.partial(kernel, n_group, n_dp), out_shape=(jax.S...  23.8 us
    pallas_call x1, Pallas kernels, per_device(): pl.pallas_call(update, out_shape=(jax.ShapeDtypeStruct(table.shape, BF),...  1.69 us

profile of v5, /device:TPU:0, one launch (start us, length us, event | category | flops | bytes accessed | tf_op | source)
XLA Modules:
  0.0 26.1 jit_solution(14138077576327085787)
XLA Ops:
  0.6 23.8 %bags.1 = (bf16[32,16,128]{2,1,0:T(8,128)(2,1)S(1)}, bf16[512,64]{1,0:T(8,128)(2,1)S(1)}, f32[4,128]{1,0:T(4,128)S(1)}, bf16[512,1024]{1,0:T(8,128)(2,1)S(1)}) custom-call(s32[1,32]{1,0:T(1,128)} %bitcast.5, s32[1,32]{1,0:T(1,128)} %bitcast.6, bf16[32,128]{1,0:T(8,128)(2,1)} %w_hbm.1, bf16[4,1024]{1,0:T(4,128)(2,1)} %cot_hbm.1, f32[4,128]{1,0:T(4,128)} %bitcast.4, ...), custom_call_target="tpu_custom_call" | custom-call | tf_op jit(solution)/shard_map/bags/pallas_call | solution.py:356
  24.4 1.7 %update.1 = (bf16[512,1024]{1,0:T(8,128)(2,1)}, f32[4,128]{1,0:T(4,128)}) custom-call(bf16[512,64]{1,0:T(8,128)(2,1)S(1)} %get-tuple-element.8.dense_t, bf16[32,16,128]{2,1,0:T(8,128)(2,1)S(1)} %get-tuple-element.9.tiles, f32[4,128]{1,0:T(4,128)S(1)} %get-tuple-element.10.accum, bf16[512,1024]{1,0:T(8,128)(2,1)S(1)} %get-tuple-element.11.table), custom_call_target="tpu_custom_call" | custom-call | tf_op jit(solution)/shard_map/update/pallas_call | solution.py:402

commit v6 on v5

--- a/solution.py
+++ b/solution.py
@@ -81,6 +81,7 @@
     w_ref,
     cot_ref,
     hid,
+    hid_t,
     send_w,
     got_w,
     send_part,
@@ -259,6 +260,9 @@
     dense_t[...] = dense[...].astype(F32).T.astype(BF)
     load_accum.wait()
     load_hid.wait()
+    for i in range(hid.shape[0] // LANES):
+        some = pl.ds(i * LANES, LANES)
+        hid_t[:, some] = hid[some, :].T
     arrived(got_part, 1)
 
     def bag_of(g):
@@ -279,7 +283,7 @@
     pre = dot(unit.astype(BF), hid[...])
     sig = jax.nn.sigmoid(pre)
     dpre = (cot * sig * (1.0 + pre * (1.0 - sig))).astype(BF)
-    dunit = dot_nt(dpre, hid[...])
+    dunit = dot(dpre, hid_t[...])
     dbag = (dunit - unit * jnp.mean(dunit * unit, axis=-1, keepdims=True)) * inv
     dstack = jnp.concatenate(
         [dbag[:, c * LANES : (c + 1) * LANES] for c in range(chunks)], axis=0
@@ -369,6 +373,7 @@
             pltpu.VMEM(pair_weight.shape, BF),
             pltpu.VMEM(hidden_cot.shape, BF),
             pltpu.VMEM(w_hidden.shape, BF),
+            pltpu.VMEM(w_hidden.shape[::-1], BF),
             pltpu.VMEM((n, CAP, block_rows), F32),
             pltpu.VMEM((n, CAP, block_rows), F32),
             tiles,

time: 26.3 us -> 26 us (0.989)
  Pallas kernels: 25.5 us -> 25.2 us
where the time goes in v6:
time: 26 us; the launch traced here: 25.9 us
  Pallas kernels  25.2 us (97%)
  between operations  0.64 us (2%)
    pallas_call x1, Pallas kernels, per_device(): pl.pallas_call(functools.partial(kernel, n_group, n_dp), out_shape=(jax.S...  23.5 us
    pallas_call x1, Pallas kernels, per_device(): pl.pallas_call(update, out_shape=(jax.ShapeDtypeStruct(table.shape, BF),...  1.68 us

profile of v6, /device:TPU:0, one launch (start us, length us, event | category | flops | bytes accessed | tf_op | source)
XLA Modules:
  0.0 25.9 jit_solution(11663952634865088169)
XLA Ops:
  0.6 23.5 %bags.1 = (bf16[32,16,128]{2,1,0:T(8,128)(2,1)S(1)}, bf16[512,64]{1,0:T(8,128)(2,1)S(1)}, f32[4,128]{1,0:T(4,128)S(1)}, bf16[512,1024]{1,0:T(8,128)(2,1)S(1)}) custom-call(s32[1,32]{1,0:T(1,128)} %bitcast.5, s32[1,32]{1,0:T(1,128)} %bitcast.6, bf16[32,128]{1,0:T(8,128)(2,1)} %w_hbm.1, bf16[4,1024]{1,0:T(4,128)(2,1)} %cot_hbm.1, f32[4,128]{1,0:T(4,128)} %bitcast.4, ...), custom_call_target="tpu_custom_call" | custom-call | tf_op jit(solution)/shard_map/bags/pallas_call | solution.py:360
  24.2 1.7 %update.1 = (bf16[512,1024]{1,0:T(8,128)(2,1)}, f32[4,128]{1,0:T(4,128)}) custom-call(bf16[512,64]{1,0:T(8,128)(2,1)S(1)} %get-tuple-element.8.dense_t, bf16[32,16,128]{2,1,0:T(8,128)(2,1)S(1)} %get-tuple-element.9.tiles, f32[4,128]{1,0:T(4,128)S(1)} %get-tuple-element.10.accum, bf16[512,1024]{1,0:T(8,128)(2,1)S(1)} %get-tuple-element.11.table), custom_call_target="tpu_custom_call" | custom-call | tf_op jit(solution)/shard_map/update/pallas_call | solution.py:407

commit v7 on v6

--- a/solution.py
+++ b/solution.py
@@ -36,6 +36,16 @@
 
 def rest(x, k):
     return jnp.bitwise_and(x, k - 1)
+
+
+def flips(x, count):
+    found = [x]
+    k = 1
+    while k < count:
+        change = k * (1 - 2 * lax.rem(lax.div(x, k), 2))
+        found += [y + change for y in found]
+        k *= 2
+    return found
 
 
 def ones_where(mask):
@@ -109,10 +119,9 @@
 
     def to_all(act):
         if n <= 32:
-            at_group = [lax.rem(mine[0] + a, n_group) for a in range(n_group)]
-            at_dp = [lax.rem(mine[1] + b, n_dp) for b in range(n_dp)]
-            for b in sorted(range(n_dp), key=lambda b: -min(b, n_dp - b)):
-                for a in range(n_group):
+            at_group, at_dp = flips(mine[0], n_group), flips(mine[1], n_dp)
+            for a in reversed(range(n_group)):
+                for b in reversed(range(n_dp)):
                     if a or b:
                         act((at_group[a], at_dp[b]), at_group[a] * n_dp + at_dp[b])
         else:

time: 26 us -> 25.1 us (0.965)
  Pallas kernels: 25.2 us -> 24.3 us
    pallas_call x1, Pallas kernels: 23.5 us -> 22.6 us  [per_device(): pl.pallas_call(functools.partial(kernel, n_group, n_dp), out_shape=(jax.S...]
where the time goes in v7:
time: 25.1 us; the launch traced here: 25 us
  Pallas kernels  24.3 us (97%)
  between operations  0.64 us (3%)
    pallas_call x1, Pallas kernels, per_device(): pl.pallas_call(functools.partial(kernel, n_group, n_dp), out_shape=(jax.S...  22.6 us
    pallas_call x1, Pallas kernels, per_device(): pl.pallas_call(update, out_shape=(jax.ShapeDtypeStruct(table.shape, BF),...  1.68 us

profile of v7, /device:TPU:0, one launch (start us, length us, event | category | flops | bytes accessed | tf_op | source)
XLA Modules:
  0.0 25.0 jit_solution(8300246847168261198)
XLA Ops:
  0.6 22.6 %bags.1 = (bf16[32,16,128]{2,1,0:T(8,128)(2,1)S(1)}, bf16[512,64]{1,0:T(8,128)(2,1)S(1)}, f32[4,128]{1,0:T(4,128)S(1)}, bf16[512,1024]{1,0:T(8,128)(2,1)S(1)}) custom-call(s32[1,32]{1,0:T(1,128)} %bitcast.5, s32[1,32]{1,0:T(1,128)} %bitcast.6, bf16[32,128]{1,0:T(8,128)(2,1)} %w_hbm.1, bf16[4,1024]{1,0:T(4,128)(2,1)} %cot_hbm.1, f32[4,128]{1,0:T(4,128)} %bitcast.4, ...), custom_call_target="tpu_custom_call" | custom-call | tf_op jit(solution)/shard_map/bags/pallas_call | solution.py:369
  23.3 1.7 %update.1 = (bf16[512,1024]{1,0:T(8,128)(2,1)}, f32[4,128]{1,0:T(4,128)}) custom-call(bf16[512,64]{1,0:T(8,128)(2,1)S(1)} %get-tuple-element.8.dense_t, bf16[32,16,128]{2,1,0:T(8,128)(2,1)S(1)} %get-tuple-element.9.tiles, f32[4,128]{1,0:T(4,128)S(1)} %get-tuple-element.10.accum, bf16[512,1024]{1,0:T(8,128)(2,1)S(1)} %get-tuple-element.11.table), custom_call_target="tpu_custom_call" | custom-call | tf_op jit(solution)/shard_map/update/pallas_call | solution.py:416

commit v8 on v7

--- a/solution.py
+++ b/solution.py
@@ -120,10 +120,12 @@
     def to_all(act):
         if n <= 32:
             at_group, at_dp = flips(mine[0], n_group), flips(mine[1], n_dp)
+            half = n_dp // 2
             for a in reversed(range(n_group)):
-                for b in reversed(range(n_dp)):
-                    if a or b:
-                        act((at_group[a], at_dp[b]), at_group[a] * n_dp + at_dp[b])
+                for b in reversed(range(half)):
+                    for c in (b + half, b):
+                        if a or c:
+                            act((at_group[a], at_dp[c]), at_group[a] * n_dp + at_dp[c])
         else:
 
             def one(i, carry):

time: 25.1 us -> 25 us (level)
  no operation moved by 1% of the time
where the time goes in v8:
time: 25 us; the launch traced here: 24.9 us
  Pallas kernels  24.2 us (97%)
  between operations  0.64 us (3%)
    pallas_call x1, Pallas kernels, per_device(): pl.pallas_call(functools.partial(kernel, n_group, n_dp), out_shape=(jax.S...  22.6 us
    pallas_call x1, Pallas kernels, per_device(): pl.pallas_call(update, out_shape=(jax.ShapeDtypeStruct(table.shape, BF),...  1.68 us

profile of v8, /device:TPU:0, one launch (start us, length us, event | category | flops | bytes accessed | tf_op | source)
XLA Modules:
  0.0 24.9 jit_solution(8297413732758974469)
XLA Ops:
  0.6 22.6 %bags.1 = (bf16[32,16,128]{2,1,0:T(8,128)(2,1)S(1)}, bf16[512,64]{1,0:T(8,128)(2,1)S(1)}, f32[4,128]{1,0:T(4,128)S(1)}, bf16[512,1024]{1,0:T(8,128)(2,1)S(1)}) custom-call(s32[1,32]{1,0:T(1,128)} %bitcast.5, s32[1,32]{1,0:T(1,128)} %bitcast.6, bf16[32,128]{1,0:T(8,128)(2,1)} %w_hbm.1, bf16[4,1024]{1,0:T(4,128)(2,1)} %cot_hbm.1, f32[4,128]{1,0:T(4,128)} %bitcast.4, ...), custom_call_target="tpu_custom_call" | custom-call | tf_op jit(solution)/shard_map/bags/pallas_call | solution.py:371
  23.2 1.7 %update.1 = (bf16[512,1024]{1,0:T(8,128)(2,1)}, f32[4,128]{1,0:T(4,128)}) custom-call(bf16[512,64]{1,0:T(8,128)(2,1)S(1)} %get-tuple-element.8.dense_t, bf16[32,16,128]{2,1,0:T(8,128)(2,1)S(1)} %get-tuple-element.9.tiles, f32[4,128]{1,0:T(4,128)S(1)} %get-tuple-element.10.accum, bf16[512,1024]{1,0:T(8,128)(2,1)S(1)} %get-tuple-element.11.table), custom_call_target="tpu_custom_call" | custom-call | tf_op jit(solution)/shard_map/update/pallas_call | solution.py:418

commit v9 on v8

--- a/solution.py
+++ b/solution.py
@@ -86,6 +86,7 @@
     dense_t,
     accum,
     table,
+    unpack,
     blk_ref,
     prot_ref,
     w_ref,
@@ -98,6 +99,7 @@
     got_part,
     send_grad,
     dense,
+    part,
     pick,
     pick_t,
     sends,
@@ -112,16 +114,16 @@
     copies = [
         pltpu.make_async_copy(a, b, loads.at[i]) for i, (a, b) in enumerate(pairs_of + others_of)
     ]
-    for copy in copies:
+    for copy in copies[:3]:
         copy.start()
     load_pairs = copies[:3]
     load_table, load_hid, load_cot, load_accum = copies[3:]
 
-    def to_all(act):
+    def to_all(act, sides=range(n_group)):
         if n <= 32:
             at_group, at_dp = flips(mine[0], n_group), flips(mine[1], n_dp)
             half = n_dp // 2
-            for a in reversed(range(n_group)):
+            for a in reversed(sides):
                 for b in reversed(range(half)):
                     for c in (b + half, b):
                         if a or c:
@@ -142,9 +144,12 @@
         )
     )
 
-    def exchange(send, got, phase):
-        to_all(
-            lambda device, t: pltpu.make_async_remote_copy(
+    for copy in copies[3:]:
+        copy.start()
+
+    def exchange(send, got, phase, make=None):
+        def start(device, t):
+            pltpu.make_async_remote_copy(
                 src_ref=send.at[t],
                 dst_ref=got.at[me],
                 send_sem=sends.at[phase],
@@ -152,7 +157,18 @@
                 device_id=device,
                 device_id_type=MESH,
             ).start()
-        )
+
+        if make is None:
+            to_all(start)
+        elif n <= 32 and groups == 2:
+            half = lax.div(me, step)
+            make(1 - half)
+            to_all(start, range(n_group // 2, n_group))
+            make(half)
+            to_all(start, range(n_group // 2))
+        else:
+            each(make)
+            to_all(start)
         got[me] = send[me]
 
     others = pl.ds(0, n - 1)
@@ -184,7 +200,8 @@
             lax.fori_loop(0, groups, lambda g, c: (body(g), c)[1], 0)
 
     def at(g, size):
-        return pl.ds(g * size, size) if few else pl.ds(pl.multiple_of(g * size, size), size)
+        fixed = isinstance(g, int)
+        return pl.ds(g * size, size) if fixed else pl.ds(pl.multiple_of(g * size, size), size)
 
     for copy in load_pairs:
         copy.wait()
@@ -233,7 +250,7 @@
     each(make_pick)
 
     stacked = step * CAP
-    pack, _ = repack(step, chunks)
+    pack, unpack[...] = repack(step, chunks)
     arrived(got_w, 0)
 
     def make_dense(g):
@@ -247,26 +264,24 @@
     each(make_dense)
     load_table.wait()
     big = min(slots, 256)
-    per_big = big // stacked
-
-    def make_part(h):
-        some = dense[pl.ds(h * big if few else pl.multiple_of(h * big, big), big), :]
-        part = dot(some, table[...]).astype(BF)
-        for j in range(per_big):
-            own = part[j * stacked : (j + 1) * stacked]
-            stack = jnp.concatenate(
-                [own[:, c * LANES : (c + 1) * LANES] for c in range(chunks)], axis=0
-            )
-            send_part[at(h * per_big + j, step)] = (
-                dot(pack, stack).astype(BF).reshape(step, tile, LANES)
-            )
+
+    def multiply(h):
+        part[at(h, big), :] = dot(dense[at(h, big), :], table[...]).astype(BF)
 
     if few:
         for h in range(slots // big):
-            make_part(h)
+            multiply(h)
     else:
-        lax.fori_loop(0, slots // big, lambda h, c: (make_part(h), c)[1], 0)
-    exchange(send_part, got_part, 1)
+        lax.fori_loop(0, slots // big, lambda h, c: (multiply(h), c)[1], 0)
+
+    def make_part(g):
+        own = part[at(g, stacked), :]
+        stack = jnp.concatenate(
+            [own[:, c * LANES : (c + 1) * LANES] for c in range(chunks)], axis=0
+        )
+        send_part[at(g, step)] = dot(pack, stack).astype(BF).reshape(step, tile, LANES)
+
+    exchange(send_part, got_part, 1, make_part)
 
     dense_t[...] = dense[...].astype(F32).T.astype(BF)
     load_accum.wait()
@@ -305,15 +320,16 @@
             dot(pick_t[at(g, rows), :], dstack).astype(BF).reshape(step, tile, LANES)
         )
 
-    each(make_grad)
-    exchange(send_grad, got_grad, 2)
+    exchange(send_grad, got_grad, 2, make_grad)
     left(send_w, 0)
     left(send_part, 1)
     left(send_grad, 2)
     arrived(got_grad, 2)
 
 
-def update(dense_t, tiles, accum, table, out_hbm, acc_hbm, rows_out, acc_out, gathered, stores):
+def update(
+    dense_t, tiles, accum, table, unpack, out_hbm, acc_hbm, rows_out, acc_out, gathered, stores
+):
     n, tile, _ = tiles.shape
     blocks, block_rows = accum.shape
     chunks = tile // CAP
@@ -321,13 +337,12 @@
     groups = n // step
     stacked = step * CAP
     parts = [pl.ds(b * block_rows, block_rows) for b in range(blocks)]
-    _, unpack = repack(step, chunks)
     diagonal = iota((block_rows, block_rows), 0) == iota((block_rows, block_rows), 1)
 
     def make_gathered(g):
         few = groups <= 4
         gathered[pl.ds(g * stacked if few else pl.multiple_of(g * stacked, stacked), stacked), :] = (
-            unpacked(unpack, tiles[pl.ds(g * step, step)], chunks)
+            unpacked(unpack[...], tiles[pl.ds(g * step, step)], chunks)
         )
 
     if groups <= 4:
@@ -368,16 +383,17 @@
     vmem = pl.BlockSpec(memory_space=pltpu.VMEM)
     tiles = pltpu.VMEM((n, tile, LANES), BF)
     stack = (width // LANES) * PAD
-    got_grad, dense_t, accum_held, table_held = pl.pallas_call(
+    got_grad, dense_t, accum_held, table_held, unpack = pl.pallas_call(
         functools.partial(kernel, n_group, n_dp),
         out_shape=(
             jax.ShapeDtypeStruct((n, tile, LANES), BF),
             jax.ShapeDtypeStruct((rows_dev, slots), BF),
             jax.ShapeDtypeStruct((blocks, block_rows), F32),
             jax.ShapeDtypeStruct(table.shape, BF),
+            jax.ShapeDtypeStruct((step * tile, step * tile), BF),
         ),
         in_specs=[hbm] * 7,
-        out_specs=(vmem,) * 4,
+        out_specs=(vmem,) * 5,
         scratch_shapes=[
             pltpu.VMEM((1, pairs), jnp.int32),
             pltpu.VMEM((1, pairs), jnp.int32),
@@ -391,6 +407,7 @@
             tiles,
             tiles,
             pltpu.VMEM((slots, rows_dev), BF),
+            pltpu.VMEM((slots, width), BF),
             pltpu.VMEM((n // step, stack, step * tile), BF),
             pltpu.VMEM((n * tile, stack), BF),
             pltpu.SemaphoreType.DMA((3,)),
@@ -421,7 +438,7 @@
             jax.ShapeDtypeStruct(table.shape, BF),
             jax.ShapeDtypeStruct((blocks, block_rows), F32),
         ),
-        in_specs=[vmem] * 4,
+        in_specs=[vmem] * 5,
         out_specs=(hbm, hbm),
         scratch_shapes=[
             pltpu.VMEM(table.shape, BF),
@@ -431,7 +448,7 @@
         ],
         compiler_params=pltpu.CompilerParams(vmem_limit_bytes=LIMIT // 2),
         name="update",
-    )(dense_t, got_grad, accum_held, table_held)
+    )(dense_t, got_grad, accum_held, table_held, unpack)
     return new_table, new_accum.reshape(rows_dev)
 
 

time: 25 us -> 25 us (level)
  no operation moved by 1% of the time
where the time goes in v9:
time: 25 us; the launch traced here: 24.9 us
  Pallas kernels  24.2 us (97%)
  between operations  0.64 us (3%)
    pallas_call x1, Pallas kernels, per_device(): pl.pallas_call(functools.partial(kernel, n_group, n_dp), out_shape=(jax.S...  22.5 us
    pallas_call x1, Pallas kernels, per_device(): pl.pallas_call(update, out_shape=(jax.ShapeDtypeStruct(table.shape, BF),...  1.67 us

profile of v9, /device:TPU:0, one launch (start us, length us, event | category | flops | bytes accessed | tf_op | source)
XLA Modules:
  0.0 24.9 jit_solution(4322660478271922055)
XLA Ops:
  0.6 22.5 %bags.1 = (bf16[32,16,128]{2,1,0:T(8,128)(2,1)S(1)}, bf16[512,64]{1,0:T(8,128)(2,1)S(1)}, f32[4,128]{1,0:T(4,128)S(1)}, bf16[512,1024]{1,0:T(8,128)(2,1)S(1)}, bf16[256,256]{1,0:T(8,128)(2,1)S(1)}) custom-call(s32[1,32]{1,0:T(1,128)} %bitcast.5, s32[1,32]{1,0:T(1,128)} %bitcast.6, bf16[32,128]{1,0:T(8,128)(2,1)} %w_hbm.1, bf16[4,1024]{1,0:T(4,128)(2,1)} %cot_hbm.1, ...), custom_call_target="tpu_custom_call" | custom-call | tf_op jit(solution)/shard_map/bags/pallas_call | solution.py:386
  23.2 1.7 %update.1 = (bf16[512,1024]{1,0:T(8,128)(2,1)}, f32[4,128]{1,0:T(4,128)}) custom-call(bf16[512,64]{1,0:T(8,128)(2,1)S(1)} %get-tuple-element.9.dense_t, bf16[32,16,128]{2,1,0:T(8,128)(2,1)S(1)} %get-tuple-element.10.tiles, f32[4,128]{1,0:T(4,128)S(1)} %get-tuple-element.11.accum, bf16[512,1024]{1,0:T(8,128)(2,1)S(1)} %get-tuple-element.12.table, ...), custom_call_target="tpu_custom_call" | custom-call | tf_op jit(solution)/shard_map/update/pallas_call | solution.py:435

commit v10 on v9

--- a/solution.py
+++ b/solution.py
@@ -147,28 +147,32 @@
     for copy in copies[3:]:
         copy.start()
 
-    def exchange(send, got, phase, make=None):
+    halves = n <= 32 and n == 2 * TOGETHER
+    half = lax.div(me, TOGETHER)
+    far_sides, near_sides = range(n_group // 2, n_group), range(n_group // 2)
+
+    def sending(send, got, phase, landed):
         def start(device, t):
             pltpu.make_async_remote_copy(
                 src_ref=send.at[t],
                 dst_ref=got.at[me],
                 send_sem=sends.at[phase],
-                recv_sem=recvs.at[phase],
+                recv_sem=recvs.at[landed],
                 device_id=device,
                 device_id_type=MESH,
             ).start()
 
-        if make is None:
-            to_all(start)
-        elif n <= 32 and groups == 2:
-            half = lax.div(me, step)
+        return start
+
+    def exchange(send, got, phase, make):
+        if halves:
             make(1 - half)
-            to_all(start, range(n_group // 2, n_group))
+            to_all(sending(send, got, phase, phase), far_sides)
             make(half)
-            to_all(start, range(n_group // 2))
+            to_all(sending(send, got, phase, phase), near_sides)
         else:
             each(make)
-            to_all(start)
+            to_all(sending(send, got, phase, phase))
         got[me] = send[me]
 
     others = pl.ds(0, n - 1)
@@ -234,7 +238,12 @@
 
     each(make_w)
     pl.semaphore_wait(barrier, n - 1)
-    exchange(send_w, got_w, 0)
+    if halves:
+        to_all(sending(send_w, got_w, 0, 0), far_sides)
+        to_all(sending(send_w, got_w, 0, 3), near_sides)
+    else:
+        to_all(sending(send_w, got_w, 0, 0))
+    got_w[me] = send_w[me]
 
     for_prot = ones_where(rest(iota((chunks * PAD, pairs), 0), PAD) == local_prot)
     shape = (chunks * PAD, rows)
@@ -251,8 +260,6 @@
 
     stacked = step * CAP
     pack, unpack[...] = repack(step, chunks)
-    arrived(got_w, 0)
-
     def make_dense(g):
         marked = got_w[at(g, step)].reshape(stacked, block_rows)
         plain = marked.astype(BF).astype(F32)
@@ -261,18 +268,10 @@
             axis=1,
         ).astype(BF)
 
-    each(make_dense)
-    load_table.wait()
-    big = min(slots, 256)
+    big = stacked if halves else min(slots, 256)
 
     def multiply(h):
         part[at(h, big), :] = dot(dense[at(h, big), :], table[...]).astype(BF)
-
-    if few:
-        for h in range(slots // big):
-            multiply(h)
-    else:
-        lax.fori_loop(0, slots // big, lambda h, c: (multiply(h), c)[1], 0)
 
     def make_part(g):
         own = part[at(g, stacked), :]
@@ -281,7 +280,24 @@
         )
         send_part[at(g, step)] = dot(pack, stack).astype(BF).reshape(step, tile, LANES)
 
-    exchange(send_part, got_part, 1, make_part)
+    load_table.wait()
+    if halves:
+        for g, sides, landed, count in (
+            (1 - half, far_sides, 0, step),
+            (half, near_sides, 3, step - 1),
+        ):
+            some = got_w.at[pl.ds(0, count)]
+            pltpu.make_async_copy(some, some, recvs.at[landed]).wait()
+            make_dense(g)
+            multiply(g)
+            make_part(g)
+            to_all(sending(send_part, got_part, 1, 1), sides)
+        got_part[me] = send_part[me]
+    else:
+        arrived(got_w, 0)
+        each(make_dense)
+        lax.fori_loop(0, slots // big, lambda h, c: (multiply(h), c)[1], 0)
+        exchange(send_part, got_part, 1, make_part)
 
     dense_t[...] = dense[...].astype(F32).T.astype(BF)
     load_accum.wait()
@@ -411,7 +427,7 @@
             pltpu.VMEM((n // step, stack, step * tile), BF),
             pltpu.VMEM((n * tile, stack), BF),
             pltpu.SemaphoreType.DMA((3,)),
-            pltpu.SemaphoreType.DMA((3,)),
+            pltpu.SemaphoreType.DMA((4,)),
             pltpu.SemaphoreType.DMA((7,)),
         ],
         compiler_params=pltpu.CompilerParams(

time: 25 us -> 24.8 us (level)
  no operation moved by 1% of the time
where the time goes in v10:
time: 24.8 us; the launch traced here: 24.6 us
  Pallas kernels  24 us (97%)
  between operations  0.64 us (3%)
    pallas_call x1, Pallas kernels, per_device(): pl.pallas_call(functools.partial(kernel, n_group, n_dp), out_shape=(jax.S...  22.3 us
    pallas_call x1, Pallas kernels, per_device(): pl.pallas_call(update, out_shape=(jax.ShapeDtypeStruct(table.shape, BF),...  1.68 us

profile of v10, /device:TPU:0, one launch (start us, length us, event | category | flops | bytes accessed | tf_op | source)
XLA Modules:
  0.0 24.6 jit_solution(15328204593981766373)
XLA Ops:
  0.6 22.3 %bags.1 = (bf16[32,16,128]{2,1,0:T(8,128)(2,1)S(1)}, bf16[512,64]{1,0:T(8,128)(2,1)S(1)}, f32[4,128]{1,0:T(4,128)S(1)}, bf16[512,1024]{1,0:T(8,128)(2,1)S(1)}, bf16[256,256]{1,0:T(8,128)(2,1)S(1)}) custom-call(s32[1,32]{1,0:T(1,128)} %bitcast.5, s32[1,32]{1,0:T(1,128)} %bitcast.6, bf16[32,128]{1,0:T(8,128)(2,1)} %w_hbm.1, bf16[4,1024]{1,0:T(4,128)(2,1)} %cot_hbm.1, ...), custom_call_target="tpu_custom_call" | custom-call | tf_op jit(solution)/shard_map/bags/pallas_call | solution.py:402
  22.9 1.7 %update.1 = (bf16[512,1024]{1,0:T(8,128)(2,1)}, f32[4,128]{1,0:T(4,128)}) custom-call(bf16[512,64]{1,0:T(8,128)(2,1)S(1)} %get-tuple-element.9.dense_t, bf16[32,16,128]{2,1,0:T(8,128)(2,1)S(1)} %get-tuple-element.10.tiles, f32[4,128]{1,0:T(4,128)S(1)} %get-tuple-element.11.accum, bf16[512,1024]{1,0:T(8,128)(2,1)S(1)} %get-tuple-element.12.table, ...), custom_call_target="tpu_custom_call" | custom-call | tf_op jit(solution)/shard_map/update/pallas_call | solution.py:451

commit v11 on v10

--- a/solution.py
+++ b/solution.py
@@ -122,10 +122,10 @@
     def to_all(act, sides=range(n_group)):
         if n <= 32:
             at_group, at_dp = flips(mine[0], n_group), flips(mine[1], n_dp)
-            half = n_dp // 2
-            for a in reversed(sides):
-                for b in reversed(range(half)):
-                    for c in (b + half, b):
+            middle = n_dp // 2
+            for b in reversed(range(middle)):
+                for a in reversed(sides):
+                    for c in (b + middle, b):
                         if a or c:
                             act((at_group[a], at_dp[c]), at_group[a] * n_dp + at_dp[c])
         else:

time: 24.8 us -> 24.7 us (level)
  no operation moved by 1% of the time
where the time goes in v11:
time: 24.7 us; the launch traced here: 24.6 us
  Pallas kernels  23.9 us (97%)
  between operations  0.64 us (3%)
    pallas_call x1, Pallas kernels, per_device(): pl.pallas_call(functools.partial(kernel, n_group, n_dp), out_shape=(jax.S...  22.2 us
    pallas_call x1, Pallas kernels, per_device(): pl.pallas_call(update, out_shape=(jax.ShapeDtypeStruct(table.shape, BF),...  1.67 us

profile of v11, /device:TPU:0, one launch (start us, length us, event | category | flops | bytes accessed | tf_op | source)
XLA Modules:
  0.0 24.6 jit_solution(16205835071924240298)
XLA Ops:
  0.6 22.2 %bags.1 = (bf16[32,16,128]{2,1,0:T(8,128)(2,1)S(1)}, bf16[512,64]{1,0:T(8,128)(2,1)S(1)}, f32[4,128]{1,0:T(4,128)S(1)}, bf16[512,1024]{1,0:T(8,128)(2,1)S(1)}, bf16[256,256]{1,0:T(8,128)(2,1)S(1)}) custom-call(s32[1,32]{1,0:T(1,128)} %bitcast.5, s32[1,32]{1,0:T(1,128)} %bitcast.6, bf16[32,128]{1,0:T(8,128)(2,1)} %w_hbm.1, bf16[4,1024]{1,0:T(4,128)(2,1)} %cot_hbm.1, ...), custom_call_target="tpu_custom_call" | custom-call | tf_op jit(solution)/shard_map/bags/pallas_call | solution.py:402
  22.9 1.7 %update.1 = (bf16[512,1024]{1,0:T(8,128)(2,1)}, f32[4,128]{1,0:T(4,128)}) custom-call(bf16[512,64]{1,0:T(8,128)(2,1)S(1)} %get-tuple-element.9.dense_t, bf16[32,16,128]{2,1,0:T(8,128)(2,1)S(1)} %get-tuple-element.10.tiles, f32[4,128]{1,0:T(4,128)S(1)} %get-tuple-element.11.accum, bf16[512,1024]{1,0:T(8,128)(2,1)S(1)} %get-tuple-element.12.table, ...), custom_call_target="tpu_custom_call" | custom-call | tf_op jit(solution)/shard_map/update/pallas_call | solution.py:451
